TPU v7x, 512 devices: a whole 4x8x8 slice. The times are simulated.
512 devices in a mesh: inst: 64 (over x, z, y_hi), tp: 8 (over y_lo, core).
Axes of the slice: x: 4, y: 8 (y_hi: 2, y_lo: 4; y = y_hi * 4 + y_lo), z: 8, core: 2. Of those that a mesh axis runs over, the one named last changes fastest.
Arguments:
- queries: bfloat16 [1024, 8192], P(('inst', 'tp')), may hold values from -32 to 32
- new_kv: bfloat16 [1024, 2048], P(('inst', 'tp')), may hold values from -6 to 6
- kv_pool: bfloat16 [64, 256, 16, 8, 256], P('inst', None, None, 'tp'), may hold values from -8 to 8
- context_lens: int32 [1024], P('inst'), may hold values from 1 to 256, 131072 in all
- block_table: int32 [1024, 16], P('inst'), may hold values from 0 to 255, as said below
- send_pages: int32 [64, 64], P('inst'), may hold values from 0 to 255
- send_dest: int32 [4096, 1], P('inst'), may hold values from 0 to 63; in each aligned block of 64 rows (0 to 63, 64 to 127, ...) at most 2 rows name the same one
- recv_pool: bfloat16 [64, 128, 16, 8, 256], P('inst', None, None, 'tp'), may hold values from -6 to 6
- recv_table: int32 [64, 128], P('inst'), may hold values from 0 to 127, each once within a row
Outputs:
- attended: bfloat16 [1024, 8192], P(('inst', 'tp'))
- landed_pool: bfloat16 [64, 128, 16, 8, 256], P('inst', None, None, 'tp')
Inputs may be any that keep to these rules, and one draw needn't show every extreme that they name: `context_lens`: some row has exactly 256 cached tokens. `block_table`: the entries of one instance's rows are pairwise distinct. `send_dest`: among one source's 64 listed pages at most 2 go to any one destination, and in some source's list exactly 2 go to one destination. `recv_table`: each instance's row is a permutation of its receiving slots.
All inputs are finite; a program needn't handle non-finite values. No bound on the sum of `context_lens` on one device may be relied on, other than what follows from the above.
Results may differ from a plain program's by a relative error of at most 0.007.
Values may be sent and summed in bfloat16 or wider, within the bound.
No kernel may reach another device: no remote copies, remote signals or barrier semaphores. Data moves between devices by JAX's collectives and lax.ppermute only.
A program may use at most 64 MiB of HBM per device.

v0:
```python
import jax
import jax.numpy as jnp
from jax import lax
from jax.sharding import PartitionSpec as P


def land_pages(kv_pool, send_pages, send_dest, recv_pool, recv_table):
    peers = lax.axis_size("inst")
    listed = send_pages.shape[1]
    capacity = recv_table.shape[1] // peers
    target_inst = send_dest[:, 0]
    listed_index = jnp.arange(listed)
    earlier_same = (target_inst[:, None] == target_inst[None, :]) & (
        listed_index[None, :] < listed_index[:, None]
    )
    position = jnp.sum(earlier_same.astype(jnp.int32), axis=1)
    moved = kv_pool[0][send_pages[0]]
    outgoing = (
        jnp.zeros((peers, capacity) + moved.shape[1:], moved.dtype)
        .at[target_inst, position]
        .set(moved)
    )
    filled = jnp.zeros((peers, capacity), jnp.bfloat16).at[target_inst, position].set(1.0)
    arrived, present = (
        lax.all_to_all(outgoing, "inst", split_axis=0, concat_axis=0, tiled=True),
        lax.all_to_all(filled, "inst", split_axis=0, concat_axis=0, tiled=True),
    )
    slot_table = recv_table[0].reshape(peers, capacity)
    target_slot = jnp.where(present > 0, slot_table, recv_table.shape[1])
    new_pool = (
        recv_pool[0]
        .at[target_slot.reshape(-1)]
        .set(arrived.reshape((-1,) + moved.shape[1:]), mode="drop")
    )
    return new_pool[None]


def on_device(
    queries,
    new_kv,
    kv_pool,
    context_lens,
    block_table,
    send_pages,
    send_dest,
    recv_pool,
    recv_table,
):
    groups = lax.axis_size("tp")
    local_rows = queries.shape[0]
    head_dim = kv_pool.shape[-1] // 2
    kv_local = kv_pool.shape[3]
    heads_local = queries.shape[1] // groups // head_dim
    group_size = heads_local // kv_local
    score_scale = head_dim ** (-0.5)
    query_split = queries.reshape(local_rows, groups, heads_local * head_dim)
    fresh_split = new_kv.reshape(local_rows, groups, kv_local * 2 * head_dim)
    query_heads, fresh_heads = (
        lax.all_to_all(query_split, "tp", split_axis=1, concat_axis=0, tiled=True),
        lax.all_to_all(fresh_split, "tp", split_axis=1, concat_axis=0, tiled=True),
    )
    inst_rows = query_heads.shape[0]
    row_block = 8
    blocks = inst_rows // row_block
    pool_local = kv_pool[0]
    tokens_all = block_table.shape[1] * pool_local.shape[1]
    query_blocks = query_heads.reshape(blocks, row_block, kv_local, group_size, head_dim)
    fresh_blocks = fresh_heads.reshape(blocks, row_block, kv_local, 2 * head_dim)
    length_blocks = context_lens.reshape(blocks, row_block)
    table_blocks = block_table.reshape(blocks, row_block, block_table.shape[1])

    def attend_block(inputs):
        query_blk, fresh_blk, length_blk, table_blk = inputs
        cache = pool_local[table_blk].reshape(row_block, tokens_all, kv_local, 2 * head_dim)
        cache_keys = cache[..., :head_dim]
        cache_values = cache[..., head_dim:]
        scores = (
            jnp.einsum("bgjd,btgd->bgjt", query_blk, cache_keys, preferred_element_type=jnp.float32)
            * score_scale
        )
        own_score = (
            jnp.einsum(
                "bgjd,bgd->bgj",
                query_blk,
                fresh_blk[..., :head_dim],
                preferred_element_type=jnp.float32,
            )
            * score_scale
        )
        live = (jnp.arange(tokens_all)[None, :] < length_blk[:, None])[:, None, None, :]
        row_max = jnp.maximum(jnp.max(jnp.where(live, scores, -1e30), axis=-1), own_score)
        weights_raw = jnp.where(live, jnp.exp(scores - row_max[..., None]), 0.0)
        own_raw = jnp.exp(own_score - row_max)
        weight_sum = jnp.sum(weights_raw, axis=-1) + own_raw
        weights = (weights_raw / weight_sum[..., None]).astype(jnp.bfloat16)
        own_weight = (own_raw / weight_sum).astype(jnp.bfloat16)
        mixed_out = jnp.einsum(
            "bgjt,btgd->bgjd", weights, cache_values, preferred_element_type=jnp.float32
        )
        mixed_out = mixed_out + own_weight.astype(jnp.float32)[..., None] * fresh_blk[
            :, :, None, head_dim:
        ].astype(jnp.float32)
        return mixed_out.astype(jnp.bfloat16)

    mixed = lax.map(attend_block, (query_blocks, fresh_blocks, length_blocks, table_blocks))
    mixed = mixed.reshape(inst_rows, heads_local * head_dim)
    attended = lax.all_to_all(mixed, "tp", split_axis=0, concat_axis=1, tiled=True)
    landed_pool = land_pages(kv_pool, send_pages, send_dest, recv_pool, recv_table)
    return (attended, landed_pool)


def solution(mesh):
    return jax.shard_map(
        on_device,
        mesh=mesh,
        in_specs=(
            P(("inst", "tp"), None),
            P(("inst", "tp"), None),
            P("inst", None, None, "tp", None),
            P("inst"),
            P("inst", None),
            P("inst", None),
            P("inst", None),
            P("inst", None, None, "tp", None),
            P("inst", None),
        ),
        out_specs=(P(("inst", "tp"), None), P("inst", None, None, "tp", None)),
        check_vma=False,
    )
```

profile of v0, /device:TPU:8, one launch (start us, length us, event | category | flops | bytes accessed | tf_op | source)
XLA Modules:
  0.0 111.7 jit_solution(654896685033943861)
XLA Ops:
  0.7 9.2 %all-to-all-start.1 = ((bf16[2,8,256]{2,0,1:T(2,128)(2,1)}), bf16[2,8,256]{2,0,1:T(2,128)(2,1)S(1)}, u32[]{:S(2)}, u32[]{:S(2)}) async-start(bf16[2,8,256]{2,0,1:T(2,128)(2,1)} %bitcast.19), calls=%async_computation.1 | async-start | bytes 16384 | tf_op jit(solution)/shard_map/all_to_all | solution.py:60
  9.9 0.2 convert_reduce_fusion
  10.1 4.0 %all-to-all-done.1 = bf16[2,8,256]{2,0,1:T(2,128)(2,1)S(1)} async-done(((bf16[2,8,256]{2,0,1:T(2,128)(2,1)}), bf16[2,8,256]{2,0,1:T(2,128)(2,1)S(1)}, u32[]{:S(2)}, u32[]{:S(2)}) %all-to-all-start.1) | async-done | bytes 8224 | tf_op jit(solution)/shard_map/all_to_all | solution.py:60
  14.1 4.7 %all-to-all-start = ((bf16[2,8,1024]{2,0,1:T(2,128)(2,1)}), bf16[2,8,1024]{2,0,1:T(2,128)(2,1)S(1)}, u32[]{:S(2)}, u32[]{:S(2)}) async-start(bf16[2,8,1024]{2,0,1:T(2,128)(2,1)} %bitcast.14), calls=%async_computation | async-start | bytes 65536 | tf_op jit(solution)/shard_map/all_to_all | solution.py:59
  18.8 3.6 %scatter_fusion = bf16[64,2]{0,1:T(2,128)(2,1)S(1)} fusion(bf16[64,2]{0,1:T(2,128)(2,1)S(1)} %broadcast.128, s32[64]{0:T(128)S(1)} %fusion.25, bf16[64]{0:T(256)(128)(2,1)S(1)} %broadcast.165), kind=kCustom, calls=%fused_computation.2 | custom fusion | bytes 896 | tf_op jit(solution)/shard_map/scatter | solution.py:23
  22.4 0.7 copy.24
  23.1 0.1 reshape.232
  23.2 13.7 %all-to-all-start.3 = ((bf16[64,1,2]{2,1,0:T(2,128)(2,1)}), bf16[64,1,2]{2,1,0:T(2,128)(2,1)S(1)}, u32[]{:S(2)}, u32[]{:S(2)}) async-start(bf16[64,1,2]{2,1,0:T(2,128)(2,1)} %copy.24), calls=%async_computation.3 | async-start | bytes 65536 | tf_op jit(solution)/shard_map/all_to_all | solution.py:26
  37.0 3.5 %while.10 = (s32[]{:T(128)}, bf16[2,8,1,8,128]{4,3,1,2,0:T(8,128)(2,1)S(1)}, s32[2,8]{1,0:T(2,128)S(1)}, bf16[2,8,1,8,128]{4,3,1,2,0:T(8,128)(2,1)S(1)}, s32[2,8...) while((s32[]{:T(128)}, ...), condition=%wide.region_3.4_spmd, body=%wide.region_0.3_spmd.sunk | while | flops 8598338 | bytes 3446989 | solution.py:105
  37.1 0.6 gather_fusion
  37.8 0.3 select_reduce_fusion.2
  38.2 0.1 fusion.38
  38.3 0.2 fusion.39
  38.5 0.2 fusion.41
  38.9 0.6 gather_fusion
  39.6 0.3 select_reduce_fusion.2
  39.9 0.1 fusion.38
  40.1 0.2 fusion.39
  40.3 0.2 fusion.41
  40.5 0.6 all_to_all.51
  41.2 9.9 %all-to-all-done.3 = bf16[64,1,2]{2,1,0:T(2,128)(2,1)S(1)} async-done(((bf16[64,1,2]{2,1,0:T(2,128)(2,1)}), bf16[64,1,2]{2,1,0:T(2,128)(2,1)S(1)}, u32[]{:S(2)}, u32[]{:S(2)}) %all-to-all-start.3) | async-done | bytes 288 | tf_op jit(solution)/shard_map/all_to_all | solution.py:26
  51.1 5.1 %all-to-all-start.2 = ((bf16[8,2,1024]{2,1,0:T(2,128)(2,1)}), bf16[8,2,1024]{2,1,0:T(2,128)(2,1)S(1)}, u32[]{:S(2)}, u32[]{:S(2)}) async-start(bf16[8,2,1024]{2,1,0:T(2,128)(2,1)} %all_to_all.51), calls=%async_computation.2 | async-start | bytes 65536 | tf_op jit(solution)/shard_map/all_to_all | solution.py:107
  56.2 1.4 %gather_fusion.1 = bf16[64,16,256]{2,1,0:T(8,128)(2,1)} fusion(bf16[256,16,256]{2,1,0:T(8,128)(2,1)S(1)} %bitcast.112, s32[1024]{0:T(1024)S(1)} %pad_clamp_fusion.1), kind=kCustom, calls=%fused_computation.1 | custom fusion | bytes 1048832 | tf_op jit(solution)/shard_map/gather | solution.py:17
  57.6 1.1 broadcast.166
  58.7 8.1 %scatter_fusion.1 = bf16[64,2,16,256]{3,2,1,0:T(8,128)(2,1)} fusion(bf16[64,2,16,256]{3,2,1,0:T(8,128)(2,1)} %broadcast.166, s32[64]{0:T(128)S(1)} %fusion.25, bf16[64,16,256]{2,1,0:T(8,128)(2,1)} %gather_fusion.1), kind=kCustom, calls=%fused_computation.3 | custom fusion | bytes 1573376 | tf_op jit(solution)/shard_map/scatter | solution.py:21
  66.8 5.2 %all-to-all-start.4 = ((bf16[64,2,16,1,256]{4,2,1,3,0:T(8,128)(2,1)}), bf16[64,2,16,1,256]{4,2,1,3,0:T(8,128)(2,1)S(1)}, u32[]{:S(2)}, u32[]{:S(2)}) async-start(bf16[64,2,16,1,256]{4,2,1,3,0:T(8,128)(2,1)} %bitcast.34), calls=%async_computation.4 | async-start | bytes 2097152 | tf_op jit(solution)/shard_map/all_to_all | solution.py:25
  72.0 0.1 compare_reduce_fusion
  72.1 0.1 gt.15
  72.3 33.9 %all-to-all-done.4 = bf16[64,2,16,1,256]{4,2,1,3,0:T(8,128)(2,1)S(1)} async-done(((bf16[64,2,16,1,256]{4,2,1,3,0:T(8,128)(2,1)}), bf16[64,2,16,1,256]{4,2,1,3,0:T(8,128)(2,1)S(1)}, u32[]{:S(2)}, u32[]{:S(2)}) %all-to-all-start.4) | async-done | bytes 1048608 | tf_op jit(solution)/shard_map/all_to_all | solution.py:25
  106.2 4.5 %scatter_fusion.2 = bf16[128,16,256]{2,1,0:T(8,128)(2,1)S(1)} fusion(bf16[128,16,256]{2,1,0:T(8,128)(2,1)S(1)} %bitcast.114, s32[128]{0:T(128)S(1)} %fusion.23, bf16[128,16,256]{2,1,0:T(8,128)(2,1)S(1)} %bitcast.115), kind=kCustom, calls=%fused_computation.4 | custom fusion | bytes 3146240 | tf_op jit(solution)/shard_map/scatter | solution.py:33
  110.7 0.7 copy.46
  111.4 0.3 copy-done.1
  (44 shorter events, 0.5 us)
Async XLA Ops:
  0.6 36.3 %copy-start = (bf16[1,256,16,1,256]{4,2,3,1,0:T(8,128)(2,1)S(1)}, bf16[1,256,16,1,256]{4,2,3,1,0:T(8,128)(2,1)}, u32[]{:S(2)}) copy-start(bf16[1,256,16,1,256]{4,2,3,1,0:T(8,128)(2,1)} %param.13) | copy-start | bytes 6291460
  0.6 22.5 %copy-start.6 = (s32[16]{0:T(128)S(1)}, s32[16]{0:T(128)}, u32[]{:S(2)}) copy-start(s32[16]{0:T(128)} %param.14) | copy-start | bytes 196
  0.7 36.3 %copy-start.3 = (s32[16,16]{1,0:T(8,128)S(1)}, s32[16,16]{1,0:T(8,128)}, u32[]{:S(2)}) copy-start(s32[16,16]{1,0:T(8,128)} %param.15) | copy-start | bytes 3076
  0.7 18.1 %copy-start.5 = (s32[1,64]{1,0:T(1,128)S(1)}, s32[1,64]{1,0:T(1,128)}, u32[]{:S(2)}) copy-start(s32[1,64]{1,0:T(1,128)} %param.16) | copy-start | bytes 772
  0.7 9.2 %copy-start.4 = (s32[64,1]{0,1:T(1,128)S(1)}, s32[64,1]{0,1:T(1,128)}, u32[]{:S(2)}) copy-start(s32[64,1]{0,1:T(1,128)} %param.17) | copy-start | bytes 772
  0.7 13.4 %all-to-all-start.1 = ((bf16[2,8,256]{2,0,1:T(2,128)(2,1)}), bf16[2,8,256]{2,0,1:T(2,128)(2,1)S(1)}, u32[]{:S(2)}, u32[]{:S(2)}) async-start(bf16[2,8,256]{2,0,1:T(2,128)(2,1)} %bitcast.19), calls=%async_computation.1 | async-start | bytes 16384 | tf_op jit(solution)/shard_map/all_to_all | solution.py:60
  14.1 9.1 %all-to-all-start = ((bf16[2,8,1024]{2,0,1:T(2,128)(2,1)}), bf16[2,8,1024]{2,0,1:T(2,128)(2,1)S(1)}, u32[]{:S(2)}, u32[]{:S(2)}) async-start(bf16[2,8,1024]{2,0,1:T(2,128)(2,1)} %bitcast.14), calls=%async_computation | async-start | bytes 65536 | tf_op jit(solution)/shard_map/all_to_all | solution.py:59
  23.2 27.9 %all-to-all-start.3 = ((bf16[64,1,2]{2,1,0:T(2,128)(2,1)}), bf16[64,1,2]{2,1,0:T(2,128)(2,1)S(1)}, u32[]{:S(2)}, u32[]{:S(2)}) async-start(bf16[64,1,2]{2,1,0:T(2,128)(2,1)} %copy.24), calls=%async_computation.3 | async-start | bytes 65536 | tf_op jit(solution)/shard_map/all_to_all | solution.py:26
  51.1 15.7 %all-to-all-start.2 = ((bf16[8,2,1024]{2,1,0:T(2,128)(2,1)}), bf16[8,2,1024]{2,1,0:T(2,128)(2,1)S(1)}, u32[]{:S(2)}, u32[]{:S(2)}) async-start(bf16[8,2,1024]{2,1,0:T(2,128)(2,1)} %all_to_all.51), calls=%async_computation.2 | async-start | bytes 65536 | tf_op jit(solution)/shard_map/all_to_all | solution.py:107
  58.7 13.6 %copy-start.7 = (s32[1,128]{1,0:T(1,128)S(1)}, s32[1,128]{1,0:T(1,128)}, u32[]{:S(2)}) copy-start(s32[1,128]{1,0:T(1,128)} %param.19) | copy-start | bytes 1540
  58.7 47.5 %copy-start.2 = (bf16[1,128,16,1,256]{4,2,3,1,0:T(8,128)(2,1)S(1)}, bf16[1,128,16,1,256]{4,2,3,1,0:T(8,128)(2,1)}, u32[]{:S(2)}) copy-start(bf16[1,128,16,1,256]{4,2,3,1,0:T(8,128)(2,1)} %param.18) | copy-start | bytes 3145732
  66.8 39.4 %all-to-all-start.4 = ((bf16[64,2,16,1,256]{4,2,1,3,0:T(8,128)(2,1)}), bf16[64,2,16,1,256]{4,2,1,3,0:T(8,128)(2,1)S(1)}, u32[]{:S(2)}, u32[]{:S(2)}) async-start(bf16[64,2,16,1,256]{4,2,1,3,0:T(8,128)(2,1)} %bitcast.34), calls=%async_computation.4 | async-start | bytes 2097152 | tf_op jit(solution)/shard_map/all_to_all | solution.py:25
  110.7 1.0 copy-start.1
where the time goes:
time: 112 us
  waiting for transfers between devices  47.8 us (43%)
  starting transfers between devices  37.9 us (34%)
  local copies, waits for them, and re-layouts  22.8 us (20%)
  matrix products  1.4 us (1%)
    all_to_all x1, waiting for transfers between devices, land_pages(): lax.all_to_all(outgoing, 'inst', split_axis=0, concat_axis=0, tiled=True)  33.9 us
    all_to_all x1, starting transfers between devices, land_pages(): lax.all_to_all(filled, 'inst', split_axis=0, concat_axis=0, tiled=True)  13.7 us
    all_to_all x1, waiting for transfers between devices, land_pages(): lax.all_to_all(filled, 'inst', split_axis=0, concat_axis=0, tiled=True)  9.93 us
    all_to_all x1, starting transfers between devices, on_device(): lax.all_to_all(fresh_split, 'tp', split_axis=1, concat_axis=0, tiled=True)  9.21 us
    scatter x1, local copies, waits for them, and re-layouts, land_pages(): outgoing = jnp.zeros((peers, capacity) + moved.shape[1:], moved.dtype).at...  8.07 us
    all_to_all x1, starting transfers between devices, land_pages(): lax.all_to_all(outgoing, 'inst', split_axis=0, concat_axis=0, tiled=True)  5.2 us
    all_to_all x1, starting transfers between devices, on_device(): lax.all_to_all(mixed, 'tp', split_axis=0, concat_axis=1, tiled=True)  5.12 us
    all_to_all x1, starting transfers between devices, on_device(): lax.all_to_all(query_split, 'tp', split_axis=1, concat_axis=0, tiled=True)  4.69 us
  transfers between devices with their start and end apart: 5, of which 3 were waited for; matrix products, arithmetic and copies ran while one was open for 17% of the time, Pallas kernels for 0%

commit v1 on v0

v1 whole, which is shorter than its diff:
```python
import functools

import jax
import jax.numpy as jnp
from jax import lax
from jax.experimental import pallas as pl
from jax.experimental.pallas import tpu as pltpu
from jax.sharding import PartitionSpec as P

EMPTY = 256.0
EDGE = 64.0
MASKED = -1e30


def pack_kernel(capacity, pages_ref, dest_ref, pool_ref, out_ref, pages, dest, taken, packed, sems):
    listed = dest.shape[1]
    peers = taken.shape[0]
    lists = (
        pltpu.make_async_copy(pages_ref, pages, sems.at[0]),
        pltpu.make_async_copy(dest_ref, dest, sems.at[1]),
    )
    for copy in lists:
        copy.start()
    packed[...] = jnp.full(packed.shape, EMPTY, packed.dtype)

    def clear(peer, carry):
        taken[peer] = 0
        return carry

    lax.fori_loop(0, peers, clear, 0, unroll=8)
    for copy in lists:
        copy.wait()

    def send(index, carry):
        peer = dest[0, index]
        position = taken[peer]
        taken[peer] = position + 1
        pltpu.make_async_copy(
            pool_ref.at[pages[0, index]], packed.at[peer * capacity + position], sems.at[2]
        ).start()
        return carry

    lax.fori_loop(0, listed, send, 0, unroll=8)
    pltpu.make_async_copy(
        pool_ref.at[pl.ds(0, listed)], packed.at[pl.ds(0, listed)], sems.at[2]
    ).wait()
    done = pltpu.make_async_copy(packed, out_ref, sems.at[0])
    done.start()
    done.wait()


def pack_pages(pool, pages, dest, peers, capacity):
    page_shape = pool.shape[1:]
    listed = dest.shape[1]
    packed_shape = (peers * capacity,) + page_shape
    return pl.pallas_call(
        functools.partial(pack_kernel, capacity),
        out_shape=jax.ShapeDtypeStruct(packed_shape, pool.dtype),
        in_specs=[
            pl.BlockSpec(memory_space=pl.ANY),
            pl.BlockSpec(memory_space=pl.ANY),
            pl.BlockSpec(memory_space=pltpu.HBM),
        ],
        out_specs=pl.BlockSpec(memory_space=pl.ANY),
        scratch_shapes=[
            pltpu.SMEM((1, listed), jnp.int32),
            pltpu.SMEM((1, listed), jnp.int32),
            pltpu.SMEM((peers,), jnp.int32),
            pltpu.VMEM(packed_shape, pool.dtype),
            pltpu.SemaphoreType.DMA((3,)),
        ],
        name="pack_pages",
    )(pages, dest, pool)


def stage_kernel(from_ref, to_ref, sem):
    copy = pltpu.make_async_copy(from_ref, to_ref, sem)
    copy.start()
    copy.wait()


def stage(x):
    return pl.pallas_call(
        stage_kernel,
        out_shape=pltpu.VMEM(x.shape, x.dtype),
        in_specs=[pl.BlockSpec(memory_space=pltpu.HBM)],
        out_specs=pl.BlockSpec(memory_space=pltpu.VMEM),
        scratch_shapes=[pltpu.SemaphoreType.DMA],
        compiler_params=pltpu.CompilerParams(vmem_limit_bytes=16 * 1024 * 1024),
        name="stage_old_pages",
    )(x)


def land_kernel(source_ref, arrived_ref, old_ref, out_ref, landed, sems):
    slots = landed.shape[0]
    parts = sems.shape[0]
    step = slots // parts
    copies = []
    for part in range(parts):

        def place(slot, carry):
            page = arrived_ref[source_ref[slot]]
            landed[slot] = jnp.where(page > EDGE, old_ref[slot], page)
            return carry

        lax.fori_loop(part * step, (part + 1) * step, place, 0, unroll=True)
        copies.append(
            pltpu.make_async_copy(
                landed.at[pl.ds(part * step, step)],
                out_ref.at[pl.ds(part * step, step)],
                sems.at[part],
            )
        )
        copies[-1].start()
    for copy in copies:
        copy.wait()


def land_pages(arrived, old, source):
    return pl.pallas_call(
        land_kernel,
        out_shape=jax.ShapeDtypeStruct(old.shape, old.dtype),
        in_specs=[
            pl.BlockSpec(memory_space=pltpu.SMEM),
            pl.BlockSpec(memory_space=pltpu.VMEM),
            pl.BlockSpec(memory_space=pltpu.VMEM),
        ],
        out_specs=pl.BlockSpec(memory_space=pl.ANY),
        scratch_shapes=[
            pltpu.VMEM(old.shape, old.dtype),
            pltpu.SemaphoreType.DMA((8,)),
        ],
        compiler_params=pltpu.CompilerParams(vmem_limit_bytes=16 * 1024 * 1024),
        name="land_pages",
    )(source, arrived, old)


def attend_kernel(scale, query_ref, fresh_ref, owner_ref, pool_ref, out_ref, score_ref):
    rows = query_ref.shape[0]
    dim = fresh_ref.shape[1] // 2
    group = query_ref.shape[1] // dim
    lanes = owner_ref.shape[1]
    chunk = 4 * lanes
    tokens = pool_ref.shape[0]
    query = jnp.concatenate([query_ref[:, j * dim : (j + 1) * dim] for j in range(group)], axis=0)
    fresh_key = jnp.concatenate([fresh_ref[:, :dim].astype(jnp.float32)] * group, axis=0)
    fresh_value = jnp.concatenate([fresh_ref[:, dim:].astype(jnp.float32)] * group, axis=0)
    own = jnp.sum(query.astype(jnp.float32) * fresh_key, axis=1, keepdims=True) * scale
    row_of = lax.broadcasted_iota(jnp.int32, (group * rows, lanes), 0) % rows
    top = jnp.full((group * rows, lanes), MASKED, jnp.float32)
    for start in range(0, tokens, chunk):
        keys = pool_ref[start : start + chunk, :dim]
        scores = (
            lax.dot_general(
                query, keys, (((1,), (1,)), ((), ())), preferred_element_type=jnp.float32
            )
            * scale
        )
        for part in range(chunk // lanes):
            block = start // lanes + part
            kept = jnp.where(
                owner_ref[block : block + 1, :] == row_of,
                scores[:, part * lanes : (part + 1) * lanes],
                MASKED,
            )
            score_ref[:, block * lanes : (block + 1) * lanes] = kept
            top = jnp.maximum(top, kept)
    top = jnp.maximum(jnp.max(top, axis=1, keepdims=True), own)
    own = jnp.exp(own - top)
    total = jnp.zeros((group * rows, lanes), jnp.float32)
    mixed = jnp.zeros((group * rows, dim), jnp.float32)
    for start in range(0, tokens, chunk):
        weights = jnp.exp(score_ref[:, start : start + chunk] - top)
        for part in range(chunk // lanes):
            total = total + weights[:, part * lanes : (part + 1) * lanes]
        mixed = mixed + jnp.dot(
            weights.astype(jnp.bfloat16),
            pool_ref[start : start + chunk, dim:],
            preferred_element_type=jnp.float32,
        )
    total = jnp.sum(total, axis=1, keepdims=True) + own
    mixed = (mixed + own.astype(jnp.bfloat16).astype(jnp.float32) * fresh_value) / total
    mixed = mixed.astype(out_ref.dtype)
    for j in range(group):
        out_ref[:, j * dim : (j + 1) * dim] = mixed[j * rows : (j + 1) * rows]


def attend(query, fresh, owner, pool, scale):
    rows, dim = query.shape[0], fresh.shape[1] // 2
    group = query.shape[1] // dim
    tokens = pool.shape[0]
    return pl.pallas_call(
        functools.partial(attend_kernel, scale),
        out_shape=jax.ShapeDtypeStruct(query.shape, query.dtype),
        in_specs=[pl.BlockSpec(memory_space=pltpu.VMEM)] * 4,
        out_specs=pl.BlockSpec(memory_space=pltpu.VMEM),
        scratch_shapes=[pltpu.VMEM((rows * group, tokens), jnp.float32)],
        compiler_params=pltpu.CompilerParams(vmem_limit_bytes=24 * 1024 * 1024),
        cost_estimate=pl.CostEstimate(
            flops=4 * rows * group * tokens * dim,
            bytes_accessed=pool.size * 2,
            transcendentals=rows * group * tokens,
        ),
        name="attend",
    )(query, fresh, owner, pool)


def token_owners(lengths, table, pages, page_size):
    rows, per_row = table.shape
    block = jnp.arange(rows * per_row, dtype=jnp.int32)
    row = block // per_row
    live = jnp.clip(
        (lengths[:, None] - jnp.arange(per_row, dtype=jnp.int32)[None, :] * page_size),
        0,
        page_size,
    ).reshape(-1)
    coded = row * (2 * page_size) + live
    page = jnp.arange(pages, dtype=jnp.int32)
    of_page = jnp.sum(
        jnp.where(table.reshape(-1)[None, :] == page[:, None], coded[None, :], 0), axis=1
    )
    per_line = 128 // page_size
    offset = jnp.arange(page_size, dtype=jnp.int32)
    of_page = of_page.reshape(pages // per_line, per_line, 1)
    owner = jnp.where(offset < of_page % (2 * page_size), of_page // (2 * page_size), -1)
    return owner.reshape(pages // per_line, 128)


def pair_gather(x):
    groups = lax.axis_size("tp")
    chips = [[2 * i, 2 * i + 1] for i in range(groups // 2)]
    return lax.all_gather(x, "tp", axis=0, tiled=False, axis_index_groups=chips)


def chip_exchange(pieces):
    groups = lax.axis_size("tp")
    chip = lax.axis_index("tp") // 2
    chips = pieces.shape[0]
    got = [lax.dynamic_index_in_dim(pieces, chip, 0, keepdims=False)]
    for k in range(1, chips):
        piece = lax.dynamic_index_in_dim(pieces, chip ^ k, 0, keepdims=False)
        got.append(lax.ppermute(piece, "tp", [(i, i ^ (2 * k)) for i in range(groups)]))
    stacked = jnp.stack(got)
    order = chip ^ jnp.arange(chips)
    return jnp.stack([lax.dynamic_index_in_dim(stacked, chip ^ k, 0, keepdims=False) for k in range(chips)])


def gather_queries(queries, new_kv):
    groups = lax.axis_size("tp")
    rows_local = queries.shape[0]
    split = jnp.concatenate([queries.reshape(rows_local, groups, -1), new_kv.reshape(rows_local, groups, -1)], axis=2)
    got = lax.all_to_all(split, "tp", split_axis=1, concat_axis=0, tiled=True)
    return got.reshape(groups * rows_local, -1)


def return_heads(mixed, me):
    groups = lax.axis_size("tp")
    rows, width = mixed.shape
    rows_local = rows // groups
    both = pair_gather(mixed)
    both = both.reshape(2, groups // 2, 2, rows_local, width)
    mine = lax.dynamic_index_in_dim(both, me % 2, 2, keepdims=False)
    got = chip_exchange(mine.transpose(1, 0, 2, 3))
    return got.reshape(groups, rows_local, width).transpose(1, 0, 2).reshape(rows_local, -1)


def on_device(
    queries,
    new_kv,
    kv_pool,
    context_lens,
    block_table,
    send_pages,
    send_dest,
    recv_pool,
    recv_table,
):
    groups = lax.axis_size("tp")
    peers = lax.axis_size("inst")
    me = lax.axis_index("tp")
    _, pages, page_size, kv_local, width = kv_pool.shape
    dim = width // 2
    heads_width = queries.shape[1] // groups
    slots = recv_table.shape[1]
    pool = kv_pool.reshape(pages, page_size, width)

    both = gather_queries(queries, new_kv)
    outgoing = pack_pages(pool, send_pages, send_dest.reshape(1, -1), peers, slots // peers)
    both, outgoing = lax.optimization_barrier((both, outgoing))
    arrived = lax.all_to_all(outgoing, "inst", split_axis=0, concat_axis=0, tiled=True)

    owner = token_owners(context_lens, block_table, pages, page_size)
    mixed = attend(
        both[:, :heads_width],
        both[:, heads_width:],
        owner,
        pool.reshape(pages * page_size, width),
        dim ** (-0.5),
    )
    attended = return_heads(mixed, me)

    slot = jnp.arange(slots, dtype=jnp.int32)
    source = jnp.sum(
        jnp.where(recv_table[0][None, :] == slot[:, None], slot[None, :], 0), axis=1
    )
    mixed, recv_pool = lax.optimization_barrier((mixed, recv_pool))
    old = stage(recv_pool.reshape(slots, page_size, width))
    landed = land_pages(arrived, old, source)
    return (attended, landed.reshape(recv_pool.shape))


def solution(mesh):
    return jax.shard_map(
        on_device,
        mesh=mesh,
        in_specs=(
            P(("inst", "tp"), None),
            P(("inst", "tp"), None),
            P("inst", None, None, "tp", None),
            P("inst"),
            P("inst", None),
            P("inst", None),
            P("inst", None),
            P("inst", None, None, "tp", None),
            P("inst", None),
        ),
        out_specs=(P(("inst", "tp"), None), P("inst", None, None, "tp", None)),
        check_vma=False,
    )
```

time: 112 us -> 65.7 us (0.59)
  waiting for transfers between devices: 47.8 us -> 19.9 us
  local copies, waits for them, and re-layouts: 22.8 us -> 2 us
  Pallas kernels: 0 us -> 5.8 us
  starting transfers between devices: 37.9 us -> 32.2 us
  blocking collectives: 0 us -> 1.85 us
  other arithmetic: 0.9 us -> 2.5 us
  matrix products: 1.4 us -> 0 us
    all_to_all x5 -> x2, waiting for transfers between devices: 47.8 us -> 12.4 us  [the longest x1 10.9 us: on_device(): lax.all_to_all(outgoing, 'inst', split_axis=0, concat_axis=0, tiled=True)]
    scatter x3 -> x0, local copies, waits for them, and re-layouts: 16.2 us -> none  [the longest x1 8.07 us: land_pages(): outgoing = jnp.zeros((peers, capacity) + moved.shape[1:], moved.dtype).at...]
    all_to_all x5 -> x2, starting transfers between devices: 37.9 us -> 22.8 us  [the longest x1 13.7 us: on_device(): lax.all_to_all(outgoing, 'inst', split_axis=0, concat_axis=0, tiled=True)]
    ppermute x0 -> x3, starting transfers between devices: none -> 9.45 us  [chip_exchange(): lax.ppermute(piece, 'tp', [(i, i ^ 2 * k) for i in range(groups)])]
    ppermute x0 -> x3, waiting for transfers between devices: none -> 7.52 us  [chip_exchange(): lax.ppermute(piece, 'tp', [(i, i ^ 2 * k) for i in range(groups)])]
    pallas_call x0 -> x4, Pallas kernels: none -> 5.8 us  [the longest x1 2.92 us: pack_pages(): pl.pallas_call(functools.partial(pack_kernel, capacity), out_shape=jax.Sh...]
    gather x3 -> x0, local copies, waits for them, and re-layouts: 2.69 us -> none  [the longest x1 1.39 us: land_pages(): moved = kv_pool[0][send_pages[0]]]
    all_gather x0 -> x1, blocking collectives: none -> 1.85 us  [pair_gather(): return lax.all_gather(x, 'tp', axis=0, tiled=False, axis_index_groups=chips)]
  transfers between devices with their start and end apart: 5 -> 5, of which waited for: 3 -> 5; matrix products, arithmetic and copies ran while one was open for 17% -> 3% of each run, Pallas kernels for 0% -> 6%
where the time goes in v1:
time: 65.7 us; the launch traced here: 65.1 us
  starting transfers between devices  32.2 us (49%)
  waiting for transfers between devices  19.9 us (30%)
  Pallas kernels  5.8 us (9%)
  other arithmetic  2.5 us (4%)
  local copies, waits for them, and re-layouts  2 us (3%)
  blocking collectives  1.85 us (3%)
  between operations  0.86 us (1%)
    all_to_all x1, starting transfers between devices, on_device(): lax.all_to_all(outgoing, 'inst', split_axis=0, concat_axis=0, tiled=True)  13.7 us
    all_to_all x1, waiting for transfers between devices, on_device(): lax.all_to_all(outgoing, 'inst', split_axis=0, concat_axis=0, tiled=True)  10.9 us
    ppermute x3, starting transfers between devices, chip_exchange(): lax.ppermute(piece, 'tp', [(i, i ^ 2 * k) for i in range(groups)])  9.45 us
    all_to_all x1, starting transfers between devices, gather_queries(): got = lax.all_to_all(split, 'tp', split_axis=1, concat_axis=0, tiled=True)  9.07 us
    ppermute x3, waiting for transfers between devices, chip_exchange(): lax.ppermute(piece, 'tp', [(i, i ^ 2 * k) for i in range(groups)])  7.52 us
    pallas_call x1, Pallas kernels, pack_pages(): pl.pallas_call(functools.partial(pack_kernel, capacity), out_shape=jax.Sh...  2.92 us
    all_gather x1, blocking collectives, pair_gather(): return lax.all_gather(x, 'tp', axis=0, tiled=False, axis_index_groups=chips)  1.85 us
    pallas_call x1, Pallas kernels, land_pages(): pl.pallas_call(land_kernel, out_shape=jax.ShapeDtypeStruct(old.shape, old...  1.58 us
  transfers between devices with their start and end apart: 5, of which 5 were waited for; matrix products, arithmetic and copies ran while one was open for 3% of the time, Pallas kernels for 6%

profile of v1, /device:TPU:8, one launch (start us, length us, event | category | flops | bytes accessed | tf_op | source)
XLA Modules:
  0.0 65.1 jit_solution(5104607906369234510)
XLA Ops:
  0.6 1.4 %pad_maximum_fusion = bf16[2,8,1280]{2,0,1:T(2,128)(2,1)} fusion(bf16[2,8,256]{2,0,1:T(2,128)(2,1)} %bitcast.44, bf16[2,8,1024]{2,0,1:T(2,128)(2,1)} %bitcast.42), kind=kLoop, calls=%fused_computation.4 | loop fusion | flops 81920 | bytes 81920 | tf_op jit(solution)/shard_map/concatenate | solution.py:251
  2.1 9.1 %all-to-all-start = ((bf16[2,8,1280]{2,0,1:T(2,128)(2,1)}), bf16[2,8,1280]{2,0,1:T(2,128)(2,1)S(1)}, u32[]{:S(2)}, u32[]{:S(2)}) async-start(bf16[2,8,1280]{2,0,1:T(2,128)(2,1)} %pad_maximum_fusion), calls=%async_computation | async-start | bytes 81920 | tf_op jit(solution)/shard_map/all_to_all | solution.py:252
  11.1 2.9 %pack_pages.1 = bf16[128,16,256]{2,1,0:T(8,128)(2,1)} custom-call(s32[1,64]{1,0:T(1,128)} %pages_ref.1, s32[1,64]{1,0:T(1,128)} %bitcast.48, bf16[256,16,256]{2,1,0:T(8,128)(2,1)} %bitcast.35), custom_call_target="tpu_custom_call" | custom-call | tf_op jit(solution)/shard_map/pack_pages/pallas_call | solution.py:56
  14.1 1.5 %all-to-all-done = bf16[2,8,1280]{2,0,1:T(2,128)(2,1)S(1)} async-done(((bf16[2,8,1280]{2,0,1:T(2,128)(2,1)}), bf16[2,8,1280]{2,0,1:T(2,128)(2,1)S(1)}, u32[]{:S(2)}, u32[]{:S(2)}) %all-to-all-start) | async-done | bytes 40992 | tf_op jit(solution)/shard_map/all_to_all | solution.py:252
  15.6 13.7 %all-to-all-start.1 = ((bf16[128,16,256]{2,1,0:T(8,128)(2,1)}), bf16[128,16,256]{2,1,0:T(8,128)(2,1)S(1)}, u32[]{:S(2)}, u32[]{:S(2)}) async-start(bf16[128,16,256]{2,1,0:T(8,128)(2,1)} %pack_pages.1), calls=%async_computation.1 | async-start | bytes 2097152 | tf_op jit(solution)/shard_map/all_to_all | solution.py:290
  29.3 0.0 copy-start.4
  29.4 0.1 eq.34
  29.5 0.1 lt.54
  29.6 0.1 subtract_clamp_fusion
  29.6 0.1 min.12
  29.7 0.1 select_reduce_fusion
  29.9 0.1 reshape.188
  30.0 0.1 copy.27
  30.0 0.1 copy.29
  30.1 0.1 copy.30
  30.2 0.1 copy.28
  30.3 1.2 %attend.1 = bf16[16,1024]{1,0:T(8,128)(2,1)S(1)} custom-call(bf16[16,1024]{1,0:T(8,128)(2,1)S(1)} %slice.6.query_ref, bf16[16,256]{1,0:T(8,128)(2,1)S(1)} %slice.7.fresh_ref, s32[32,128]{1,0:T(8,128)S(1)} %compare_select_fusion.owner_ref, bf16[4096,256]{1,0:T(8,128)(2,1)S(1)} %bitcast.36), custom_call_target="tpu_custom_call" | custom-call | flops 268435456 | bytes 2097152 | tf_op jit(solution)/shard_map/attend/pallas_call | solution.py:192
  31.5 1.9 %all-gather = bf16[32,1024]{1,0:T(8,128)(2,1)S(1)} all-gather(bf16[16,1024]{1,0:T(8,128)(2,1)S(1)} %attend.1), channel_id=2, replica_groups={{0,1},{2,3},{4,5},{6,7},{8,9},{10,11},{12,13},{14,15},{16,17},{18,19},{..., dimensions={0}, use_global_device_ids=true | all-gather | bytes 98304 | tf_op jit(solution)/shard_map/all_gather | solution.py:232
  33.5 2.4 %collective-permute-start.2 = (bf16[2,2,1024]{2,1,0:T(2,128)(2,1)S(1)}, bf16[2,2,1024]{2,1,0:T(2,128)(2,1)S(1)}, u32[]{:S(2)}, u32[]{:S(2)}) collective-permute-start(bf16[2,2,1024]{2,1,0:T(2,128)(2,1)S(1)} %get-tuple-element.15), channel_id=1, source_target_pairs={{0,6},{1,7},{2,4},{3,5},{4,2},{5,3},{6,0},{7,1},{8,14},{9,15},{10,... | collective-permute-start | bytes 24584 | tf_op jit(solution)/shard_map/ppermute | solution.py:242
  35.9 5.1 %collective-permute-start.1 = (bf16[2,2,1024]{2,1,0:T(2,128)(2,1)S(1)}, bf16[2,2,1024]{2,1,0:T(2,128)(2,1)S(1)}, u32[]{:S(2)}, u32[]{:S(2)}) collective-permute-start(bf16[2,2,1024]{2,1,0:T(2,128)(2,1)S(1)} %get-tuple-element.16), channel_id=1, source_target_pairs={{0,4},{1,5},{2,6},{3,7},{4,0},{5,1},{6,2},{7,3},{8,12},{9,13},{10,... | collective-permute-start | bytes 24584 | tf_op jit(solution)/shard_map/ppermute | solution.py:242
  41.0 1.9 %collective-permute-start = (bf16[2,2,1024]{2,1,0:T(2,128)(2,1)S(1)}, bf16[2,2,1024]{2,1,0:T(2,128)(2,1)S(1)}, u32[]{:S(2)}, u32[]{:S(2)}) collective-permute-start(bf16[2,2,1024]{2,1,0:T(2,128)(2,1)S(1)} %get-tuple-element.17), channel_id=1, source_target_pairs={{0,2},{1,3},{2,0},{3,1},{4,6},{5,7},{6,4},{7,5},{8,10},{9,11},{10,... | collective-permute-start | bytes 24584 | tf_op jit(solution)/shard_map/ppermute | solution.py:242
  42.9 0.1 select_reduce_fusion.1.source_ref
  43.0 0.0 copy-start.1
  43.1 1.2 %copy-done.1 = bf16[1,128,16,1,256]{4,2,3,1,0:T(8,128)(2,1)S(1)} copy-done((bf16[1,128,16,1,256]{4,2,3,1,0:T(8,128)(2,1)S(1)}, bf16[1,128,16,1,256]{4,2,3,1,0:T(8,128)(2,1)}, u32[]{:S(2)}) %copy-start.1) | copy-done | bytes 1048600
  44.3 0.1 stage_old_pages.1.old_ref
  44.4 0.4 collective-permute-done.2
  44.8 1.7 %collective-permute-done.1 = bf16[2,2,1024]{2,1,0:T(2,128)(2,1)S(1)} collective-permute-done((bf16[2,2,1024]{2,1,0:T(2,128)(2,1)S(1)}, bf16[2,2,1024]{2,1,0:T(2,128)(2,1)S(1)}, u32[]{:S(2)}, u32[]{:S(2)}) %collective-permute-start.1) | collective-permute-done | bytes 8224 | tf_op jit(solution)/shard_map/ppermute | solution.py:242
  46.6 5.3 %collective-permute-done = bf16[2,2,1024]{2,1,0:T(2,128)(2,1)S(1)} collective-permute-done((bf16[2,2,1024]{2,1,0:T(2,128)(2,1)S(1)}, bf16[2,2,1024]{2,1,0:T(2,128)(2,1)S(1)}, u32[]{:S(2)}, u32[]{:S(2)}) %collective-permute-start) | collective-permute-done | bytes 8224 | tf_op jit(solution)/shard_map/ppermute | solution.py:242
  51.9 0.1 pad_maximum_fusion.1
  52.0 0.7 %pad_maximum_fusion.2 = bf16[4,2,2,1024]{3,2,1,0:T(2,128)(2,1)} fusion(bf16[1,2,2,1024]{3,2,1,0:T(2,128)(2,1)S(1)} %get-tuple-element.19, bf16[1,2,2,1024]{3,2,1,0:T(2,128)(2,1)S(1)} %get-tuple-element.20, bf16[1,2,2,1024]{3,2,1,0:T(2,128)(2,1)S(1)} %get-tuple-element.21, bf16[1,2,2,1024]{3,2,1,0:T(2,128)(2,1)S(1)} %get-tuple-element.18), kind=kLoop, calls=%fused_computation.6 | loop fusion | flops 49152 | bytes 65536 | tf_op jit(solution)/shard_map/stack | solution.py:245
  52.7 10.9 %all-to-all-done.1.arrived_ref = bf16[128,16,256]{2,1,0:T(8,128)(2,1)S(1)} async-done(((bf16[128,16,256]{2,1,0:T(8,128)(2,1)}), bf16[128,16,256]{2,1,0:T(8,128)(2,1)S(1)}, u32[]{:S(2)}, u32[]{:S(2)}) %all-to-all-start.1) | async-done | bytes 1048608 | tf_op jit(solution)/shard_map/all_to_all | solution.py:290
  63.5 1.6 %land_pages.1 = bf16[128,16,256]{2,1,0:T(8,128)(2,1)} custom-call(s32[128]{0:T(128)S(1)} %select_reduce_fusion.1.source_ref, bf16[128,16,256]{2,1,0:T(8,128)(2,1)S(1)} %all-to-all-done.1.arrived_ref, bf16[128,16,256]{2,1,0:T(8,128)(2,1)S(1)} %stage_old_pages.1.old_ref), custom_call_target="tpu_custom_call" | custom-call | tf_op jit(solution)/shard_map/land_pages/pallas_call | solution.py:120
  (20 shorter events, 0.2 us)
Async XLA Ops:
  2.1 13.5 %all-to-all-start = ((bf16[2,8,1280]{2,0,1:T(2,128)(2,1)}), bf16[2,8,1280]{2,0,1:T(2,128)(2,1)S(1)}, u32[]{:S(2)}, u32[]{:S(2)}) async-start(bf16[2,8,1280]{2,0,1:T(2,128)(2,1)} %pad_maximum_fusion), calls=%async_computation | async-start | bytes 81920 | tf_op jit(solution)/shard_map/all_to_all | solution.py:252
  11.1 18.2 %copy-start.2 = (s32[16,16]{1,0:T(8,128)S(1)}, s32[16,16]{1,0:T(8,128)}, u32[]{:S(2)}) copy-start(s32[16,16]{1,0:T(8,128)} %param.13) | copy-start | bytes 3076
  11.1 18.4 %copy-start.3 = (s32[16]{0:T(128)S(1)}, s32[16]{0:T(128)}, u32[]{:S(2)}) copy-start(s32[16]{0:T(128)} %param.12) | copy-start | bytes 196
  14.1 16.2 %copy-start = (bf16[1,256,16,1,256]{4,2,3,1,0:T(8,128)(2,1)S(1)}, bf16[1,256,16,1,256]{4,2,3,1,0:T(8,128)(2,1)}, u32[]{:S(2)}) copy-start(bf16[1,256,16,1,256]{4,2,3,1,0:T(8,128)(2,1)} %param.11) | copy-start | bytes 6291460
  15.6 47.9 %all-to-all-start.1 = ((bf16[128,16,256]{2,1,0:T(8,128)(2,1)}), bf16[128,16,256]{2,1,0:T(8,128)(2,1)S(1)}, u32[]{:S(2)}, u32[]{:S(2)}) async-start(bf16[128,16,256]{2,1,0:T(8,128)(2,1)} %pack_pages.1), calls=%async_computation.1 | async-start | bytes 2097152 | tf_op jit(solution)/shard_map/all_to_all | solution.py:290
  29.3 13.6 %copy-start.4 = (s32[1,128]{1,0:T(1,128)S(1)}, s32[1,128]{1,0:T(1,128)}, u32[]{:S(2)}) copy-start(s32[1,128]{1,0:T(1,128)} %param.17) | copy-start | bytes 1540
  33.5 11.4 %collective-permute-start.2 = (bf16[2,2,1024]{2,1,0:T(2,128)(2,1)S(1)}, bf16[2,2,1024]{2,1,0:T(2,128)(2,1)S(1)}, u32[]{:S(2)}, u32[]{:S(2)}) collective-permute-start(bf16[2,2,1024]{2,1,0:T(2,128)(2,1)S(1)} %get-tuple-element.15), channel_id=1, source_target_pairs={{0,6},{1,7},{2,4},{3,5},{4,2},{5,3},{6,0},{7,1},{8,14},{9,15},{10,... | collective-permute-start | bytes 24584 | tf_op jit(solution)/shard_map/ppermute | solution.py:242
  35.9 10.6 %collective-permute-start.1 = (bf16[2,2,1024]{2,1,0:T(2,128)(2,1)S(1)}, bf16[2,2,1024]{2,1,0:T(2,128)(2,1)S(1)}, u32[]{:S(2)}, u32[]{:S(2)}) collective-permute-start(bf16[2,2,1024]{2,1,0:T(2,128)(2,1)S(1)} %get-tuple-element.16), channel_id=1, source_target_pairs={{0,4},{1,5},{2,6},{3,7},{4,0},{5,1},{6,2},{7,3},{8,12},{9,13},{10,... | collective-permute-start | bytes 24584 | tf_op jit(solution)/shard_map/ppermute | solution.py:242
  41.0 10.9 %collective-permute-start = (bf16[2,2,1024]{2,1,0:T(2,128)(2,1)S(1)}, bf16[2,2,1024]{2,1,0:T(2,128)(2,1)S(1)}, u32[]{:S(2)}, u32[]{:S(2)}) collective-permute-start(bf16[2,2,1024]{2,1,0:T(2,128)(2,1)S(1)} %get-tuple-element.17), channel_id=1, source_target_pairs={{0,2},{1,3},{2,0},{3,1},{4,6},{5,7},{6,4},{7,5},{8,10},{9,11},{10,... | collective-permute-start | bytes 24584 | tf_op jit(solution)/shard_map/ppermute | solution.py:242
  43.0 1.2 %copy-start.1 = (bf16[1,128,16,1,256]{4,2,3,1,0:T(8,128)(2,1)S(1)}, bf16[1,128,16,1,256]{4,2,3,1,0:T(8,128)(2,1)}, u32[]{:S(2)}) copy-start(bf16[1,128,16,1,256]{4,2,3,1,0:T(8,128)(2,1)} %param.16) | copy-start | bytes 3145732

commit v2 on v1

--- a/solution.py
+++ b/solution.py
@@ -10,6 +10,7 @@
 EMPTY = 256.0
 EDGE = 64.0
 MASKED = -1e30
+LEVEL_PARTS = 3
 
 
 def pack_kernel(capacity, pages_ref, dest_ref, pool_ref, out_ref, pages, dest, taken, packed, sems):
@@ -135,17 +136,14 @@
     )(source, arrived, old)
 
 
-def attend_kernel(scale, query_ref, fresh_ref, owner_ref, pool_ref, out_ref, score_ref):
+def attend_kernel(scale, query_ref, owner_ref, pool_ref, out_ref, score_ref):
     rows = query_ref.shape[0]
-    dim = fresh_ref.shape[1] // 2
+    dim = pool_ref.shape[1] // 2
     group = query_ref.shape[1] // dim
     lanes = owner_ref.shape[1]
     chunk = 4 * lanes
     tokens = pool_ref.shape[0]
     query = jnp.concatenate([query_ref[:, j * dim : (j + 1) * dim] for j in range(group)], axis=0)
-    fresh_key = jnp.concatenate([fresh_ref[:, :dim].astype(jnp.float32)] * group, axis=0)
-    fresh_value = jnp.concatenate([fresh_ref[:, dim:].astype(jnp.float32)] * group, axis=0)
-    own = jnp.sum(query.astype(jnp.float32) * fresh_key, axis=1, keepdims=True) * scale
     row_of = lax.broadcasted_iota(jnp.int32, (group * rows, lanes), 0) % rows
     top = jnp.full((group * rows, lanes), MASKED, jnp.float32)
     for start in range(0, tokens, chunk):
@@ -165,8 +163,7 @@
             )
             score_ref[:, block * lanes : (block + 1) * lanes] = kept
             top = jnp.maximum(top, kept)
-    top = jnp.maximum(jnp.max(top, axis=1, keepdims=True), own)
-    own = jnp.exp(own - top)
+    top = jnp.max(top, axis=1, keepdims=True)
     total = jnp.zeros((group * rows, lanes), jnp.float32)
     mixed = jnp.zeros((group * rows, dim), jnp.float32)
     for start in range(0, tokens, chunk):
@@ -178,21 +175,29 @@
             pool_ref[start : start + chunk, dim:],
             preferred_element_type=jnp.float32,
         )
-    total = jnp.sum(total, axis=1, keepdims=True) + own
-    mixed = (mixed + own.astype(jnp.bfloat16).astype(jnp.float32) * fresh_value) / total
-    mixed = mixed.astype(out_ref.dtype)
+    total = jnp.sum(total, axis=1, keepdims=True)
+    mixed = (mixed / total).astype(out_ref.dtype)
+    level = top + jnp.log(total)
+    lane = lax.broadcasted_iota(jnp.int32, (rows, lanes), 1)
+    levels = jnp.zeros((rows, lanes), jnp.float32)
     for j in range(group):
         out_ref[:, j * dim : (j + 1) * dim] = mixed[j * rows : (j + 1) * rows]
-
-
-def attend(query, fresh, owner, pool, scale):
-    rows, dim = query.shape[0], fresh.shape[1] // 2
+        rest = level[j * rows : (j + 1) * rows]
+        for part in range(LEVEL_PARTS):
+            piece = rest.astype(out_ref.dtype).astype(jnp.float32)
+            levels = jnp.where(lane == part * group + j, piece, levels)
+            rest = rest - piece
+    out_ref[:, group * dim :] = levels.astype(out_ref.dtype)
+
+
+def attend(query, owner, pool, scale):
+    rows, dim = query.shape[0], pool.shape[1] // 2
     group = query.shape[1] // dim
     tokens = pool.shape[0]
     return pl.pallas_call(
         functools.partial(attend_kernel, scale),
-        out_shape=jax.ShapeDtypeStruct(query.shape, query.dtype),
-        in_specs=[pl.BlockSpec(memory_space=pltpu.VMEM)] * 4,
+        out_shape=jax.ShapeDtypeStruct((rows, group * dim + 128), query.dtype),
+        in_specs=[pl.BlockSpec(memory_space=pltpu.VMEM)] * 3,
         out_specs=pl.BlockSpec(memory_space=pltpu.VMEM),
         scratch_shapes=[pltpu.VMEM((rows * group, tokens), jnp.float32)],
         compiler_params=pltpu.CompilerParams(vmem_limit_bytes=24 * 1024 * 1024),
@@ -202,7 +207,7 @@
             transcendentals=rows * group * tokens,
         ),
         name="attend",
-    )(query, fresh, owner, pool)
+    )(query, owner, pool)
 
 
 def token_owners(lengths, table, pages, page_size):
@@ -240,17 +245,15 @@
     for k in range(1, chips):
         piece = lax.dynamic_index_in_dim(pieces, chip ^ k, 0, keepdims=False)
         got.append(lax.ppermute(piece, "tp", [(i, i ^ (2 * k)) for i in range(groups)]))
-    stacked = jnp.stack(got)
-    order = chip ^ jnp.arange(chips)
-    return jnp.stack([lax.dynamic_index_in_dim(stacked, chip ^ k, 0, keepdims=False) for k in range(chips)])
-
-
-def gather_queries(queries, new_kv):
+    return got
+
+
+def gather_queries(queries):
     groups = lax.axis_size("tp")
-    rows_local = queries.shape[0]
-    split = jnp.concatenate([queries.reshape(rows_local, groups, -1), new_kv.reshape(rows_local, groups, -1)], axis=2)
+    rows = queries.shape[0]
+    split = queries.reshape(rows, groups, -1)
     got = lax.all_to_all(split, "tp", split_axis=1, concat_axis=0, tiled=True)
-    return got.reshape(groups * rows_local, -1)
+    return got.reshape(groups * rows, -1)
 
 
 def return_heads(mixed, me):
@@ -260,8 +263,62 @@
     both = pair_gather(mixed)
     both = both.reshape(2, groups // 2, 2, rows_local, width)
     mine = lax.dynamic_index_in_dim(both, me % 2, 2, keepdims=False)
-    got = chip_exchange(mine.transpose(1, 0, 2, 3))
-    return got.reshape(groups, rows_local, width).transpose(1, 0, 2).reshape(rows_local, -1)
+    return chip_exchange(mine.transpose(1, 0, 2, 3))
+
+
+def add_new_kernel(dim, scale, chip_ref, query_ref, fresh_ref, *refs):
+    pieces, out_ref = refs[:-1], refs[-1]
+    heads, _, width = pieces[0].shape
+    lanes = 128
+    group = (width - lanes) // dim
+    chip = chip_ref[0]
+    lane = lax.broadcasted_iota(jnp.int32, (pieces[0].shape[1], lanes), 1)
+    results = []
+    for k, piece in enumerate(pieces):
+        for h in range(heads):
+            place = (chip ^ k) * heads + h
+            fresh = pl.multiple_of(place * (2 * dim), 2 * dim)
+            fresh_key = fresh_ref[:, pl.ds(fresh, dim)].astype(jnp.float32)
+            fresh_value = fresh_ref[:, pl.ds(fresh + dim, dim)].astype(jnp.float32)
+            parts = piece[h, :, group * dim :].astype(jnp.float32)
+            level = parts
+            for part in range(1, LEVEL_PARTS):
+                level = level + pltpu.roll(parts, lanes - part * group, 1)
+            own = jnp.zeros_like(level)
+            places = []
+            for j in range(group):
+                places.append(pl.multiple_of(place * (group * dim) + j * dim, dim))
+                query = query_ref[:, pl.ds(places[-1], dim)].astype(jnp.float32)
+                score = jnp.sum(query * fresh_key, axis=1, keepdims=True) * scale
+                own = jnp.where(lane == j, score, own)
+            top = jnp.maximum(level, own)
+            cached, new = jnp.exp(level - top), jnp.exp(own - top)
+            total = cached + new
+            cached, new = cached / total, new / total
+            for j in range(group):
+                value = piece[h, :, j * dim : (j + 1) * dim].astype(jnp.float32)
+                mixed = value * cached[:, j : j + 1] + fresh_value * new[:, j : j + 1]
+                results.append((places[j], mixed.astype(out_ref.dtype)))
+    for at, mixed in results:
+        out_ref[:, pl.ds(at, dim)] = mixed
+
+
+def add_new_token(pieces, queries, new_kv, dim, scale):
+    chip = (lax.axis_index("tp") // 2).astype(jnp.int32).reshape(1)
+    vmem = pl.BlockSpec(memory_space=pltpu.VMEM)
+    return pl.pallas_call(
+        functools.partial(add_new_kernel, dim, scale),
+        out_shape=jax.ShapeDtypeStruct(queries.shape, queries.dtype),
+        in_specs=[pl.BlockSpec(memory_space=pltpu.SMEM)] + [vmem] * (2 + len(pieces)),
+        out_specs=vmem,
+        compiler_params=pltpu.CompilerParams(vmem_limit_bytes=16 * 1024 * 1024),
+        cost_estimate=pl.CostEstimate(
+            flops=8 * queries.size,
+            bytes_accessed=4 * queries.size,
+            transcendentals=2 * queries.size // dim,
+        ),
+        name="add_new_token",
+    )(chip, queries, new_kv, *pieces)
 
 
 def on_device(
@@ -275,29 +332,23 @@
     recv_pool,
     recv_table,
 ):
-    groups = lax.axis_size("tp")
     peers = lax.axis_size("inst")
     me = lax.axis_index("tp")
     _, pages, page_size, kv_local, width = kv_pool.shape
     dim = width // 2
-    heads_width = queries.shape[1] // groups
     slots = recv_table.shape[1]
     pool = kv_pool.reshape(pages, page_size, width)
 
-    both = gather_queries(queries, new_kv)
+    query = gather_queries(queries)
     outgoing = pack_pages(pool, send_pages, send_dest.reshape(1, -1), peers, slots // peers)
-    both, outgoing = lax.optimization_barrier((both, outgoing))
+    query, outgoing = lax.optimization_barrier((query, outgoing))
     arrived = lax.all_to_all(outgoing, "inst", split_axis=0, concat_axis=0, tiled=True)
 
     owner = token_owners(context_lens, block_table, pages, page_size)
-    mixed = attend(
-        both[:, :heads_width],
-        both[:, heads_width:],
-        owner,
-        pool.reshape(pages * page_size, width),
-        dim ** (-0.5),
-    )
-    attended = return_heads(mixed, me)
+    scale = dim ** (-0.5)
+    mixed = attend(query, owner, pool.reshape(pages * page_size, width), scale)
+    returned = return_heads(mixed, me)
+    attended = add_new_token(returned, queries, new_kv, dim, scale)
 
     slot = jnp.arange(slots, dtype=jnp.int32)
     source = jnp.sum(

time: 65.7 us -> 64.1 us (0.976)
  other arithmetic: 2.5 us -> 0.35 us
  Pallas kernels: 5.8 us -> 7.27 us
  waiting for transfers between devices: 19.9 us -> 19.1 us
    pallas_call x0 -> x1, Pallas kernels: none -> 1.56 us  [add_new_token(): pl.pallas_call(functools.partial(add_new_kernel, dim, scale), out_shape=j...]
    concatenate x1 -> x0, other arithmetic: 1.42 us -> none  [gather_queries(): jnp.concatenate([queries.reshape(rows_local, groups, -1), new_kv.reshape(...]
    all_to_all x1, waiting for transfers between devices: 10.9 us -> 10 us  [on_device(): lax.all_to_all(outgoing, 'inst', split_axis=0, concat_axis=0, tiled=True)]
    another operation x2 -> x0, other arithmetic: 0.73 us -> none  [the longest x1 0.67 us: chip_exchange(): jnp.stack([lax.dynamic_index_in_dim(stacked, chip ^ k, 0, keepdims=False)...]
  transfers between devices with their start and end apart: 5 -> 5, of which waited for: 5 -> 5; matrix products, arithmetic and copies ran while one was open for 3% -> 2% of each run, Pallas kernels for 6% -> 9%
where the time goes in v2:
time: 64.1 us; the launch traced here: 63.7 us
  starting transfers between devices  32.2 us (50%)
  waiting for transfers between devices  19.1 us (30%)
  Pallas kernels  7.27 us (11%)
  local copies, waits for them, and re-layouts  1.97 us (3%)
  blocking collectives  1.86 us (3%)
  between operations  0.85 us (1%)
    all_to_all x1, starting transfers between devices, on_device(): lax.all_to_all(outgoing, 'inst', split_axis=0, concat_axis=0, tiled=True)  13.7 us
    all_to_all x1, waiting for transfers between devices, on_device(): lax.all_to_all(outgoing, 'inst', split_axis=0, concat_axis=0, tiled=True)  10 us
    ppermute x3, starting transfers between devices, chip_exchange(): lax.ppermute(piece, 'tp', [(i, i ^ 2 * k) for i in range(groups)])  9.47 us
    all_to_all x1, starting transfers between devices, gather_queries(): got = lax.all_to_all(split, 'tp', split_axis=1, concat_axis=0, tiled=True)  9.09 us
    ppermute x3, waiting for transfers between devices, chip_exchange(): lax.ppermute(piece, 'tp', [(i, i ^ 2 * k) for i in range(groups)])  7.63 us
    pallas_call x1, Pallas kernels, pack_pages(): pl.pallas_call(functools.partial(pack_kernel, capacity), out_shape=jax.Sh...  2.9 us
    all_gather x1, blocking collectives, pair_gather(): return lax.all_gather(x, 'tp', axis=0, tiled=False, axis_index_groups=chips)  1.86 us
    pallas_call x1, Pallas kernels, land_pages(): pl.pallas_call(land_kernel, out_shape=jax.ShapeDtypeStruct(old.shape, old...  1.58 us
  transfers between devices with their start and end apart: 5, of which 5 were waited for; matrix products, arithmetic and copies ran while one was open for 2% of the time, Pallas kernels for 9%

profile of v2, /device:TPU:8, one launch (start us, length us, event | category | flops | bytes accessed | tf_op | source)
XLA Modules:
  0.0 63.7 jit_solution(6724129705181059862)
XLA Ops:
  0.6 9.1 %all-to-all-start = ((bf16[2,8,1024]{2,0,1:T(2,128)(2,1)}), bf16[2,8,1024]{2,0,1:T(2,128)(2,1)S(1)}, u32[]{:S(2)}, u32[]{:S(2)}) async-start(bf16[2,8,1024]{2,0,1:T(2,128)(2,1)} %bitcast.36), calls=%async_computation | async-start | bytes 65536 | tf_op jit(solution)/shard_map/all_to_all | solution.py:255
  9.7 2.9 %pack_pages.1 = bf16[128,16,256]{2,1,0:T(8,128)(2,1)} custom-call(s32[1,64]{1,0:T(1,128)} %pages_ref.1, s32[1,64]{1,0:T(1,128)} %bitcast.41, bf16[256,16,256]{2,1,0:T(8,128)(2,1)} %bitcast.33), custom_call_target="tpu_custom_call" | custom-call | tf_op jit(solution)/shard_map/pack_pages/pallas_call | solution.py:57
  12.6 1.5 %all-to-all-done = bf16[2,8,1024]{2,0,1:T(2,128)(2,1)S(1)} async-done(((bf16[2,8,1024]{2,0,1:T(2,128)(2,1)}), bf16[2,8,1024]{2,0,1:T(2,128)(2,1)S(1)}, u32[]{:S(2)}, u32[]{:S(2)}) %all-to-all-start) | async-done | bytes 32800 | tf_op jit(solution)/shard_map/all_to_all | solution.py:255
  14.1 0.0 copy-start.6
  14.1 13.7 %all-to-all-start.1 = ((bf16[128,16,256]{2,1,0:T(8,128)(2,1)}), bf16[128,16,256]{2,1,0:T(8,128)(2,1)S(1)}, u32[]{:S(2)}, u32[]{:S(2)}) async-start(bf16[128,16,256]{2,1,0:T(8,128)(2,1)} %pack_pages.1), calls=%async_computation.1 | async-start | bytes 2097152 | tf_op jit(solution)/shard_map/all_to_all | solution.py:345
  27.9 0.1 eq.34
  28.0 0.1 lt.50
  28.1 0.1 subtract_clamp_fusion
  28.2 0.1 min.12
  28.2 0.1 select_reduce_fusion
  28.4 0.1 reshape.183
  28.5 0.1 copy.28
  28.6 0.1 copy.30
  28.6 0.1 copy.31
  28.7 0.1 copy.29
  28.8 0.0 copy-done
  28.8 0.0 copy-start.2
  28.8 0.0 copy-start.3
  28.8 1.1 %attend.1 = bf16[16,1152]{1,0:T(8,128)(2,1)S(1)} custom-call(bf16[16,1024]{1,0:T(8,128)(2,1)S(1)} %reshape.180.query_ref, s32[32,128]{1,0:T(8,128)S(1)} %compare_select_fusion.owner_ref, bf16[4096,256]{1,0:T(8,128)(2,1)S(1)} %bitcast.34), custom_call_target="tpu_custom_call" | custom-call | flops 268435456 | bytes 2097152 | tf_op jit(solution)/shard_map/attend/pallas_call | solution.py:197
  30.0 1.9 %all-gather = bf16[32,1152]{1,0:T(8,128)(2,1)S(1)} all-gather(bf16[16,1152]{1,0:T(8,128)(2,1)S(1)} %attend.1), channel_id=2, replica_groups={{0,1},{2,3},{4,5},{6,7},{8,9},{10,11},{12,13},{14,15},{16,17},{18,19},{..., dimensions={0}, use_global_device_ids=true | all-gather | bytes 110592 | tf_op jit(solution)/shard_map/all_gather | solution.py:237
  31.9 2.5 %collective-permute-start.2 = (bf16[2,2,1152]{2,1,0:T(2,128)(2,1)S(1)}, bf16[2,2,1152]{2,1,0:T(2,128)(2,1)S(1)}, u32[]{:S(2)}, u32[]{:S(2)}) collective-permute-start(bf16[2,2,1152]{2,1,0:T(2,128)(2,1)S(1)} %get-tuple-element.14), channel_id=1, source_target_pairs={{0,6},{1,7},{2,4},{3,5},{4,2},{5,3},{6,0},{7,1},{8,14},{9,15},{10,... | collective-permute-start | bytes 27656 | tf_op jit(solution)/shard_map/ppermute | solution.py:247
  34.4 5.1 %collective-permute-start.1 = (bf16[2,2,1152]{2,1,0:T(2,128)(2,1)S(1)}, bf16[2,2,1152]{2,1,0:T(2,128)(2,1)S(1)}, u32[]{:S(2)}, u32[]{:S(2)}) collective-permute-start(bf16[2,2,1152]{2,1,0:T(2,128)(2,1)S(1)} %get-tuple-element.15), channel_id=1, source_target_pairs={{0,4},{1,5},{2,6},{3,7},{4,0},{5,1},{6,2},{7,3},{8,12},{9,13},{10,... | collective-permute-start | bytes 27656 | tf_op jit(solution)/shard_map/ppermute | solution.py:247
  39.5 1.9 %collective-permute-start = (bf16[2,2,1152]{2,1,0:T(2,128)(2,1)S(1)}, bf16[2,2,1152]{2,1,0:T(2,128)(2,1)S(1)}, u32[]{:S(2)}, u32[]{:S(2)}) collective-permute-start(bf16[2,2,1152]{2,1,0:T(2,128)(2,1)S(1)} %get-tuple-element.16), channel_id=1, source_target_pairs={{0,2},{1,3},{2,0},{3,1},{4,6},{5,7},{6,4},{7,5},{8,10},{9,11},{10,... | collective-permute-start | bytes 27656 | tf_op jit(solution)/shard_map/ppermute | solution.py:247
  41.4 0.1 select_reduce_fusion.1.source_ref
  41.6 1.2 %copy-done.1 = bf16[1,128,16,1,256]{4,2,3,1,0:T(8,128)(2,1)S(1)} copy-done((bf16[1,128,16,1,256]{4,2,3,1,0:T(8,128)(2,1)S(1)}, bf16[1,128,16,1,256]{4,2,3,1,0:T(8,128)(2,1)}, u32[]{:S(2)}) %copy-start.1) | copy-done | bytes 1048600
  42.8 0.1 stage_old_pages.1.old_ref
  42.9 2.0 %collective-permute-done.2.refs_3_ = bf16[2,2,1152]{2,1,0:T(2,128)(2,1)S(1)} collective-permute-done((bf16[2,2,1152]{2,1,0:T(2,128)(2,1)S(1)}, bf16[2,2,1152]{2,1,0:T(2,128)(2,1)S(1)}, u32[]{:S(2)}, u32[]{:S(2)}) %collective-permute-start.2) | collective-permute-done | bytes 9248 | tf_op jit(solution)/shard_map/ppermute | solution.py:247
  44.8 1.6 %collective-permute-done.1.refs_2_ = bf16[2,2,1152]{2,1,0:T(2,128)(2,1)S(1)} collective-permute-done((bf16[2,2,1152]{2,1,0:T(2,128)(2,1)S(1)}, bf16[2,2,1152]{2,1,0:T(2,128)(2,1)S(1)}, u32[]{:S(2)}, u32[]{:S(2)}) %collective-permute-start.1) | collective-permute-done | bytes 9248 | tf_op jit(solution)/shard_map/ppermute | solution.py:247
  46.4 4.1 %collective-permute-done.refs_1_ = bf16[2,2,1152]{2,1,0:T(2,128)(2,1)S(1)} collective-permute-done((bf16[2,2,1152]{2,1,0:T(2,128)(2,1)S(1)}, bf16[2,2,1152]{2,1,0:T(2,128)(2,1)S(1)}, u32[]{:S(2)}, u32[]{:S(2)}) %collective-permute-start) | collective-permute-done | bytes 9248 | tf_op jit(solution)/shard_map/ppermute | solution.py:247
  50.5 1.6 %add_new_token.1 = bf16[2,8192]{1,0:T(2,128)(2,1)} custom-call(s32[1]{0:T(128)} %bitcast.chip_ref, bf16[2,8192]{1,0:T(2,128)(2,1)S(1)} %copy-done.2, bf16[2,2048]{1,0:T(2,128)(2,1)S(1)} %copy-done.3, bf16[2,2,1152]{2,1,0:T(2,128)(2,1)S(1)} %get-tuple-element.17.refs_0_, bf16[2,2,1152]{2,1,0:T(2,128)(2,1)S(1)} %collective-permute-done.refs_1_, ...), custom_call_target="tpu_custom_call" | custom-call | flops 131072 | bytes 65536 | tf_op jit(solution)/shard_map/add_new_token/pallas_call | solution.py:309
  52.1 10.0 %all-to-all-done.1.arrived_ref = bf16[128,16,256]{2,1,0:T(8,128)(2,1)S(1)} async-done(((bf16[128,16,256]{2,1,0:T(8,128)(2,1)}), bf16[128,16,256]{2,1,0:T(8,128)(2,1)S(1)}, u32[]{:S(2)}, u32[]{:S(2)}) %all-to-all-start.1) | async-done | bytes 1048608 | tf_op jit(solution)/shard_map/all_to_all | solution.py:345
  62.1 1.6 %land_pages.1 = bf16[128,16,256]{2,1,0:T(8,128)(2,1)} custom-call(s32[128]{0:T(128)S(1)} %select_reduce_fusion.1.source_ref, bf16[128,16,256]{2,1,0:T(8,128)(2,1)S(1)} %all-to-all-done.1.arrived_ref, bf16[128,16,256]{2,1,0:T(8,128)(2,1)S(1)} %stage_old_pages.1.old_ref), custom_call_target="tpu_custom_call" | custom-call | tf_op jit(solution)/shard_map/land_pages/pallas_call | solution.py:121
  (19 shorter events, 0.2 us)
Async XLA Ops:
  0.6 13.5 %all-to-all-start = ((bf16[2,8,1024]{2,0,1:T(2,128)(2,1)}), bf16[2,8,1024]{2,0,1:T(2,128)(2,1)S(1)}, u32[]{:S(2)}, u32[]{:S(2)}) async-start(bf16[2,8,1024]{2,0,1:T(2,128)(2,1)} %bitcast.36), calls=%async_computation | async-start | bytes 65536 | tf_op jit(solution)/shard_map/all_to_all | solution.py:255
  9.7 18.2 %copy-start.4 = (s32[16,16]{1,0:T(8,128)S(1)}, s32[16,16]{1,0:T(8,128)}, u32[]{:S(2)}) copy-start(s32[16,16]{1,0:T(8,128)} %param.13) | copy-start | bytes 3076
  9.7 18.4 %copy-start.5 = (s32[16]{0:T(128)S(1)}, s32[16]{0:T(128)}, u32[]{:S(2)}) copy-start(s32[16]{0:T(128)} %param.12) | copy-start | bytes 196
  12.6 16.2 %copy-start = (bf16[1,256,16,1,256]{4,2,3,1,0:T(8,128)(2,1)S(1)}, bf16[1,256,16,1,256]{4,2,3,1,0:T(8,128)(2,1)}, u32[]{:S(2)}) copy-start(bf16[1,256,16,1,256]{4,2,3,1,0:T(8,128)(2,1)} %param.11) | copy-start | bytes 6291460
  14.1 27.3 %copy-start.6 = (s32[1,128]{1,0:T(1,128)S(1)}, s32[1,128]{1,0:T(1,128)}, u32[]{:S(2)}) copy-start(s32[1,128]{1,0:T(1,128)} %param.17) | copy-start | bytes 1540
  14.1 47.9 %all-to-all-start.1 = ((bf16[128,16,256]{2,1,0:T(8,128)(2,1)}), bf16[128,16,256]{2,1,0:T(8,128)(2,1)S(1)}, u32[]{:S(2)}, u32[]{:S(2)}) async-start(bf16[128,16,256]{2,1,0:T(8,128)(2,1)} %pack_pages.1), calls=%async_computation.1 | async-start | bytes 2097152 | tf_op jit(solution)/shard_map/all_to_all | solution.py:345
  28.8 21.7 %copy-start.2 = (bf16[2,8192]{1,0:T(2,128)(2,1)S(1)}, bf16[2,8192]{1,0:T(2,128)(2,1)}, u32[]{:S(2)}) copy-start(bf16[2,8192]{1,0:T(2,128)(2,1)} %query_ref.1) | copy-start | bytes 98308
  28.8 21.7 %copy-start.3 = (bf16[2,2048]{1,0:T(2,128)(2,1)S(1)}, bf16[2,2048]{1,0:T(2,128)(2,1)}, u32[]{:S(2)}) copy-start(bf16[2,2048]{1,0:T(2,128)(2,1)} %fresh_ref.1) | copy-start | bytes 24580
  31.9 12.9 %collective-permute-start.2 = (bf16[2,2,1152]{2,1,0:T(2,128)(2,1)S(1)}, bf16[2,2,1152]{2,1,0:T(2,128)(2,1)S(1)}, u32[]{:S(2)}, u32[]{:S(2)}) collective-permute-start(bf16[2,2,1152]{2,1,0:T(2,128)(2,1)S(1)} %get-tuple-element.14), channel_id=1, source_target_pairs={{0,6},{1,7},{2,4},{3,5},{4,2},{5,3},{6,0},{7,1},{8,14},{9,15},{10,... | collective-permute-start | bytes 27656 | tf_op jit(solution)/shard_map/ppermute | solution.py:247
  34.4 12.0 %collective-permute-start.1 = (bf16[2,2,1152]{2,1,0:T(2,128)(2,1)S(1)}, bf16[2,2,1152]{2,1,0:T(2,128)(2,1)S(1)}, u32[]{:S(2)}, u32[]{:S(2)}) collective-permute-start(bf16[2,2,1152]{2,1,0:T(2,128)(2,1)S(1)} %get-tuple-element.15), channel_id=1, source_target_pairs={{0,4},{1,5},{2,6},{3,7},{4,0},{5,1},{6,2},{7,3},{8,12},{9,13},{10,... | collective-permute-start | bytes 27656 | tf_op jit(solution)/shard_map/ppermute | solution.py:247
  39.5 11.0 %collective-permute-start = (bf16[2,2,1152]{2,1,0:T(2,128)(2,1)S(1)}, bf16[2,2,1152]{2,1,0:T(2,128)(2,1)S(1)}, u32[]{:S(2)}, u32[]{:S(2)}) collective-permute-start(bf16[2,2,1152]{2,1,0:T(2,128)(2,1)S(1)} %get-tuple-element.16), channel_id=1, source_target_pairs={{0,2},{1,3},{2,0},{3,1},{4,6},{5,7},{6,4},{7,5},{8,10},{9,11},{10,... | collective-permute-start | bytes 27656 | tf_op jit(solution)/shard_map/ppermute | solution.py:247
  41.5 1.2 %copy-start.1 = (bf16[1,128,16,1,256]{4,2,3,1,0:T(8,128)(2,1)S(1)}, bf16[1,128,16,1,256]{4,2,3,1,0:T(8,128)(2,1)}, u32[]{:S(2)}) copy-start(bf16[1,128,16,1,256]{4,2,3,1,0:T(8,128)(2,1)} %param.16) | copy-start | bytes 3145732

commit v3 on v2

--- a/solution.py
+++ b/solution.py
@@ -13,6 +13,11 @@
 LEVEL_PARTS = 3
 
 
+def place_of(inst):
+    x, z, half = inst // 16, inst // 2 % 8, inst % 2
+    return (1 - half) * 32 + (7 - z) * 4 + x
+
+
 def pack_kernel(capacity, pages_ref, dest_ref, pool_ref, out_ref, pages, dest, taken, packed, sems):
     listed = dest.shape[1]
     peers = taken.shape[0]
@@ -37,7 +42,9 @@
         position = taken[peer]
         taken[peer] = position + 1
         pltpu.make_async_copy(
-            pool_ref.at[pages[0, index]], packed.at[peer * capacity + position], sems.at[2]
+            pool_ref.at[pages[0, index]],
+            packed.at[place_of(peer) * capacity + position],
+            sems.at[2],
         ).start()
         return carry
 
@@ -342,7 +349,10 @@
     query = gather_queries(queries)
     outgoing = pack_pages(pool, send_pages, send_dest.reshape(1, -1), peers, slots // peers)
     query, outgoing = lax.optimization_barrier((query, outgoing))
-    arrived = lax.all_to_all(outgoing, "inst", split_axis=0, concat_axis=0, tiled=True)
+    order = sorted(range(peers), key=place_of)
+    arrived = lax.all_to_all(
+        outgoing, "inst", split_axis=0, concat_axis=0, tiled=True, axis_index_groups=[order]
+    )
 
     owner = token_owners(context_lens, block_table, pages, page_size)
     scale = dim ** (-0.5)
@@ -351,8 +361,10 @@
     attended = add_new_token(returned, queries, new_kv, dim, scale)
 
     slot = jnp.arange(slots, dtype=jnp.int32)
+    per_peer = slots // peers
+    where_from = place_of(slot // per_peer) * per_peer + slot % per_peer
     source = jnp.sum(
-        jnp.where(recv_table[0][None, :] == slot[:, None], slot[None, :], 0), axis=1
+        jnp.where(recv_table[0][None, :] == slot[:, None], where_from[None, :], 0), axis=1
     )
     mixed, recv_pool = lax.optimization_barrier((mixed, recv_pool))
     old = stage(recv_pool.reshape(slots, page_size, width))

time: 64.1 us -> 59.3 us (0.925)
  the two profiles are of different devices: /device:TPU:8 before, /device:TPU:48 now
where the time goes in v3:
time: 59.3 us; the launch traced here: 58.8 us
  starting transfers between devices  30.2 us (51%)
  waiting for transfers between devices  15.5 us (26%)
  Pallas kernels  7.93 us (13%)
  local copies, waits for them, and re-layouts  1.96 us (3%)
  blocking collectives  1.86 us (3%)
  between operations  0.87 us (1%)
    all_to_all x1, starting transfers between devices, on_device(): lax.all_to_all(outgoing, 'inst', split_axis=0, concat_axis=0, tiled=True,...  15.3 us
    ppermute x3, starting transfers between devices, chip_exchange(): lax.ppermute(piece, 'tp', [(i, i ^ 2 * k) for i in range(groups)])  9.56 us
    all_to_all x1, waiting for transfers between devices, on_device(): lax.all_to_all(outgoing, 'inst', split_axis=0, concat_axis=0, tiled=True,...  7.81 us
    ppermute x3, waiting for transfers between devices, chip_exchange(): lax.ppermute(piece, 'tp', [(i, i ^ 2 * k) for i in range(groups)])  7.73 us
    all_to_all x1, starting transfers between devices, gather_queries(): got = lax.all_to_all(split, 'tp', split_axis=1, concat_axis=0, tiled=True)  5.41 us
    pallas_call x1, Pallas kernels, pack_pages(): pl.pallas_call(functools.partial(pack_kernel, capacity), out_shape=jax.Sh...  3.55 us
    all_gather x1, blocking collectives, pair_gather(): return lax.all_gather(x, 'tp', axis=0, tiled=False, axis_index_groups=chips)  1.86 us
    pallas_call x1, Pallas kernels, land_pages(): pl.pallas_call(land_kernel, out_shape=jax.ShapeDtypeStruct(old.shape, old...  1.58 us
  transfers between devices with their start and end apart: 5, of which 4 were waited for; matrix products, arithmetic and copies ran while one was open for 2% of the time, Pallas kernels for 11%

profile of v3, /device:TPU:48, one launch (start us, length us, event | category | flops | bytes accessed | tf_op | source)
XLA Modules:
  0.0 58.8 jit_solution(15522690900611124864)
XLA Ops:
  0.6 5.4 %all-to-all-start = ((bf16[2,8,1024]{2,0,1:T(2,128)(2,1)}), bf16[2,8,1024]{2,0,1:T(2,128)(2,1)S(1)}, u32[]{:S(2)}, u32[]{:S(2)}) async-start(bf16[2,8,1024]{2,0,1:T(2,128)(2,1)} %bitcast.36), calls=%async_computation | async-start | bytes 65536 | tf_op jit(solution)/shard_map/all_to_all | solution.py:262
  6.0 3.6 %pack_pages.1 = bf16[128,16,256]{2,1,0:T(8,128)(2,1)} custom-call(s32[1,64]{1,0:T(1,128)} %pages_ref.1, s32[1,64]{1,0:T(1,128)} %bitcast.41, bf16[256,16,256]{2,1,0:T(8,128)(2,1)} %bitcast.33), custom_call_target="tpu_custom_call" | custom-call | tf_op jit(solution)/shard_map/pack_pages/pallas_call | solution.py:64
  9.6 0.0 copy-start
  9.7 0.0 copy-start.6
  9.7 15.3 %all-to-all-start.1 = ((bf16[128,16,256]{2,1,0:T(8,128)(2,1)}), bf16[128,16,256]{2,1,0:T(8,128)(2,1)S(1)}, u32[]{:S(2)}, u32[]{:S(2)}) async-start(bf16[128,16,256]{2,1,0:T(8,128)(2,1)} %pack_pages.1), calls=%async_computation.1 | async-start | bytes 2097152 | tf_op jit(solution)/shard_map/all_to_all | solution.py:353
  25.0 0.1 eq.38
  25.1 0.1 lt.64
  25.2 0.1 subtract_clamp_fusion
  25.3 0.1 min.12
  25.3 0.1 select_reduce_fusion
  25.5 0.1 reshape.258
  25.6 0.1 copy.28
  25.7 0.1 copy.30
  25.7 0.1 copy.31
  25.8 0.1 copy.29
  25.9 0.0 copy-start.2
  26.0 0.0 copy-start.3
  26.0 1.1 %attend.1 = bf16[16,1152]{1,0:T(8,128)(2,1)S(1)} custom-call(bf16[16,1024]{1,0:T(8,128)(2,1)S(1)} %reshape.255.query_ref, s32[32,128]{1,0:T(8,128)S(1)} %compare_select_fusion.owner_ref, bf16[4096,256]{1,0:T(8,128)(2,1)S(1)} %bitcast.34), custom_call_target="tpu_custom_call" | custom-call | flops 268435456 | bytes 2097152 | tf_op jit(solution)/shard_map/attend/pallas_call | solution.py:204
  27.1 1.9 %all-gather = bf16[32,1152]{1,0:T(8,128)(2,1)S(1)} all-gather(bf16[16,1152]{1,0:T(8,128)(2,1)S(1)} %attend.1), channel_id=2, replica_groups={{0,1},{2,3},{4,5},{6,7},{8,9},{10,11},{12,13},{14,15},{16,17},{18,19},{..., dimensions={0}, use_global_device_ids=true | all-gather | bytes 110592 | tf_op jit(solution)/shard_map/all_gather | solution.py:244
  29.1 3.1 %collective-permute-start.2 = (bf16[2,2,1152]{2,1,0:T(2,128)(2,1)S(1)}, bf16[2,2,1152]{2,1,0:T(2,128)(2,1)S(1)}, u32[]{:S(2)}, u32[]{:S(2)}) collective-permute-start(bf16[2,2,1152]{2,1,0:T(2,128)(2,1)S(1)} %get-tuple-element.14), channel_id=1, source_target_pairs={{0,6},{1,7},{2,4},{3,5},{4,2},{5,3},{6,0},{7,1},{8,14},{9,15},{10,... | collective-permute-start | bytes 27656 | tf_op jit(solution)/shard_map/ppermute | solution.py:254
  32.2 4.5 %collective-permute-start.1 = (bf16[2,2,1152]{2,1,0:T(2,128)(2,1)S(1)}, bf16[2,2,1152]{2,1,0:T(2,128)(2,1)S(1)}, u32[]{:S(2)}, u32[]{:S(2)}) collective-permute-start(bf16[2,2,1152]{2,1,0:T(2,128)(2,1)S(1)} %get-tuple-element.15), channel_id=1, source_target_pairs={{0,4},{1,5},{2,6},{3,7},{4,0},{5,1},{6,2},{7,3},{8,12},{9,13},{10,... | collective-permute-start | bytes 27656 | tf_op jit(solution)/shard_map/ppermute | solution.py:254
  36.7 1.9 %collective-permute-start = (bf16[2,2,1152]{2,1,0:T(2,128)(2,1)S(1)}, bf16[2,2,1152]{2,1,0:T(2,128)(2,1)S(1)}, u32[]{:S(2)}, u32[]{:S(2)}) collective-permute-start(bf16[2,2,1152]{2,1,0:T(2,128)(2,1)S(1)} %get-tuple-element.16), channel_id=1, source_target_pairs={{0,2},{1,3},{2,0},{3,1},{4,6},{5,7},{6,4},{7,5},{8,10},{9,11},{10,... | collective-permute-start | bytes 27656 | tf_op jit(solution)/shard_map/ppermute | solution.py:254
  38.7 0.1 select_reduce_fusion.1.source_ref
  38.8 0.0 copy-start.1
  38.8 1.2 %copy-done.1 = bf16[1,128,16,1,256]{4,2,3,1,0:T(8,128)(2,1)S(1)} copy-done((bf16[1,128,16,1,256]{4,2,3,1,0:T(8,128)(2,1)S(1)}, bf16[1,128,16,1,256]{4,2,3,1,0:T(8,128)(2,1)}, u32[]{:S(2)}) %copy-start.1) | copy-done | bytes 1048600
  40.0 0.1 stage_old_pages.1.old_ref
  40.1 2.5 %collective-permute-done.2.refs_3_ = bf16[2,2,1152]{2,1,0:T(2,128)(2,1)S(1)} collective-permute-done((bf16[2,2,1152]{2,1,0:T(2,128)(2,1)S(1)}, bf16[2,2,1152]{2,1,0:T(2,128)(2,1)S(1)}, u32[]{:S(2)}, u32[]{:S(2)}) %collective-permute-start.2) | collective-permute-done | bytes 9248 | tf_op jit(solution)/shard_map/ppermute | solution.py:254
  42.6 0.1 collective-permute-done.1.refs_2_
  42.7 5.2 %collective-permute-done.refs_1_ = bf16[2,2,1152]{2,1,0:T(2,128)(2,1)S(1)} collective-permute-done((bf16[2,2,1152]{2,1,0:T(2,128)(2,1)S(1)}, bf16[2,2,1152]{2,1,0:T(2,128)(2,1)S(1)}, u32[]{:S(2)}, u32[]{:S(2)}) %collective-permute-start) | collective-permute-done | bytes 9248 | tf_op jit(solution)/shard_map/ppermute | solution.py:254
  47.8 1.6 %add_new_token.1 = bf16[2,8192]{1,0:T(2,128)(2,1)} custom-call(s32[1]{0:T(128)} %bitcast.chip_ref, bf16[2,8192]{1,0:T(2,128)(2,1)S(1)} %copy-done.2, bf16[2,2048]{1,0:T(2,128)(2,1)S(1)} %copy-done.3, bf16[2,2,1152]{2,1,0:T(2,128)(2,1)S(1)} %get-tuple-element.17.refs_0_, bf16[2,2,1152]{2,1,0:T(2,128)(2,1)S(1)} %collective-permute-done.refs_1_, ...), custom_call_target="tpu_custom_call" | custom-call | flops 131072 | bytes 65536 | tf_op jit(solution)/shard_map/add_new_token/pallas_call | solution.py:316
  49.4 7.8 %all-to-all-done.1.arrived_ref = bf16[128,16,256]{2,1,0:T(8,128)(2,1)S(1)} async-done(((bf16[128,16,256]{2,1,0:T(8,128)(2,1)}), bf16[128,16,256]{2,1,0:T(8,128)(2,1)S(1)}, u32[]{:S(2)}, u32[]{:S(2)}) %all-to-all-start.1) | async-done | bytes 1048608 | tf_op jit(solution)/shard_map/all_to_all | solution.py:353
  57.2 1.6 %land_pages.1 = bf16[128,16,256]{2,1,0:T(8,128)(2,1)} custom-call(s32[128]{0:T(128)S(1)} %select_reduce_fusion.1.source_ref, bf16[128,16,256]{2,1,0:T(8,128)(2,1)S(1)} %all-to-all-done.1.arrived_ref, bf16[128,16,256]{2,1,0:T(8,128)(2,1)S(1)} %stage_old_pages.1.old_ref), custom_call_target="tpu_custom_call" | custom-call | tf_op jit(solution)/shard_map/land_pages/pallas_call | solution.py:128
  (20 shorter events, 0.2 us)
Async XLA Ops:
  0.6 9.0 %all-to-all-start = ((bf16[2,8,1024]{2,0,1:T(2,128)(2,1)}), bf16[2,8,1024]{2,0,1:T(2,128)(2,1)S(1)}, u32[]{:S(2)}, u32[]{:S(2)}) async-start(bf16[2,8,1024]{2,0,1:T(2,128)(2,1)} %bitcast.36), calls=%async_computation | async-start | bytes 65536 | tf_op jit(solution)/shard_map/all_to_all | solution.py:262
  6.0 19.0 %copy-start.4 = (s32[16,16]{1,0:T(8,128)S(1)}, s32[16,16]{1,0:T(8,128)}, u32[]{:S(2)}) copy-start(s32[16,16]{1,0:T(8,128)} %param.13) | copy-start | bytes 3076
  6.0 19.1 %copy-start.5 = (s32[16]{0:T(128)S(1)}, s32[16]{0:T(128)}, u32[]{:S(2)}) copy-start(s32[16]{0:T(128)} %param.12) | copy-start | bytes 196
  9.6 16.3 %copy-start = (bf16[1,256,16,1,256]{4,2,3,1,0:T(8,128)(2,1)S(1)}, bf16[1,256,16,1,256]{4,2,3,1,0:T(8,128)(2,1)}, u32[]{:S(2)}) copy-start(bf16[1,256,16,1,256]{4,2,3,1,0:T(8,128)(2,1)} %param.11) | copy-start | bytes 6291460
  9.7 29.0 %copy-start.6 = (s32[1,128]{1,0:T(1,128)S(1)}, s32[1,128]{1,0:T(1,128)}, u32[]{:S(2)}) copy-start(s32[1,128]{1,0:T(1,128)} %param.17) | copy-start | bytes 1540
  9.7 47.5 %all-to-all-start.1 = ((bf16[128,16,256]{2,1,0:T(8,128)(2,1)}), bf16[128,16,256]{2,1,0:T(8,128)(2,1)S(1)}, u32[]{:S(2)}, u32[]{:S(2)}) async-start(bf16[128,16,256]{2,1,0:T(8,128)(2,1)} %pack_pages.1), calls=%async_computation.1 | async-start | bytes 2097152 | tf_op jit(solution)/shard_map/all_to_all | solution.py:353
  25.9 21.9 %copy-start.2 = (bf16[2,8192]{1,0:T(2,128)(2,1)S(1)}, bf16[2,8192]{1,0:T(2,128)(2,1)}, u32[]{:S(2)}) copy-start(bf16[2,8192]{1,0:T(2,128)(2,1)} %query_ref.1) | copy-start | bytes 98308
  26.0 21.9 %copy-start.3 = (bf16[2,2048]{1,0:T(2,128)(2,1)S(1)}, bf16[2,2048]{1,0:T(2,128)(2,1)}, u32[]{:S(2)}) copy-start(bf16[2,2048]{1,0:T(2,128)(2,1)} %fresh_ref.1) | copy-start | bytes 24580
  29.1 13.5 %collective-permute-start.2 = (bf16[2,2,1152]{2,1,0:T(2,128)(2,1)S(1)}, bf16[2,2,1152]{2,1,0:T(2,128)(2,1)S(1)}, u32[]{:S(2)}, u32[]{:S(2)}) collective-permute-start(bf16[2,2,1152]{2,1,0:T(2,128)(2,1)S(1)} %get-tuple-element.14), channel_id=1, source_target_pairs={{0,6},{1,7},{2,4},{3,5},{4,2},{5,3},{6,0},{7,1},{8,14},{9,15},{10,... | collective-permute-start | bytes 27656 | tf_op jit(solution)/shard_map/ppermute | solution.py:254
  32.2 10.5 %collective-permute-start.1 = (bf16[2,2,1152]{2,1,0:T(2,128)(2,1)S(1)}, bf16[2,2,1152]{2,1,0:T(2,128)(2,1)S(1)}, u32[]{:S(2)}, u32[]{:S(2)}) collective-permute-start(bf16[2,2,1152]{2,1,0:T(2,128)(2,1)S(1)} %get-tuple-element.15), channel_id=1, source_target_pairs={{0,4},{1,5},{2,6},{3,7},{4,0},{5,1},{6,2},{7,3},{8,12},{9,13},{10,... | collective-permute-start | bytes 27656 | tf_op jit(solution)/shard_map/ppermute | solution.py:254
  36.7 11.1 %collective-permute-start = (bf16[2,2,1152]{2,1,0:T(2,128)(2,1)S(1)}, bf16[2,2,1152]{2,1,0:T(2,128)(2,1)S(1)}, u32[]{:S(2)}, u32[]{:S(2)}) collective-permute-start(bf16[2,2,1152]{2,1,0:T(2,128)(2,1)S(1)} %get-tuple-element.16), channel_id=1, source_target_pairs={{0,2},{1,3},{2,0},{3,1},{4,6},{5,7},{6,4},{7,5},{8,10},{9,11},{10,... | collective-permute-start | bytes 27656 | tf_op jit(solution)/shard_map/ppermute | solution.py:254
  38.8 1.2 %copy-start.1 = (bf16[1,128,16,1,256]{4,2,3,1,0:T(8,128)(2,1)S(1)}, bf16[1,128,16,1,256]{4,2,3,1,0:T(8,128)(2,1)}, u32[]{:S(2)}) copy-start(bf16[1,128,16,1,256]{4,2,3,1,0:T(8,128)(2,1)} %param.16) | copy-start | bytes 3145732

commit v4 on v3

--- a/solution.py
+++ b/solution.py
@@ -14,7 +14,7 @@
 
 
 def place_of(inst):
-    x, z, half = inst // 16, inst // 2 % 8, inst % 2
+    x, z, half = inst >> 4, (inst >> 1) & 7, inst & 1
     return (1 - half) * 32 + (7 - z) * 4 + x
 
 

time: 59.3 us -> 58.8 us (level)
  transfers between devices with their start and end apart: 5 -> 5, of which waited for: 4 -> 4; matrix products, arithmetic and copies ran while one was open for 2% -> 2% of each run, Pallas kernels for 11% -> 10%
where the time goes in v4:
time: 58.8 us; the launch traced here: 58.3 us
  starting transfers between devices  30.1 us (51%)
  waiting for transfers between devices  15.7 us (27%)
  Pallas kernels  7.44 us (13%)
  local copies, waits for them, and re-layouts  1.96 us (3%)
  blocking collectives  1.86 us (3%)
  between operations  0.86 us (1%)
    all_to_all x1, starting transfers between devices, on_device(): lax.all_to_all(outgoing, 'inst', split_axis=0, concat_axis=0, tiled=True,...  15.3 us
    ppermute x3, starting transfers between devices, chip_exchange(): lax.ppermute(piece, 'tp', [(i, i ^ 2 * k) for i in range(groups)])  9.48 us
    all_to_all x1, waiting for transfers between devices, on_device(): lax.all_to_all(outgoing, 'inst', split_axis=0, concat_axis=0, tiled=True,...  7.8 us
    ppermute x3, waiting for transfers between devices, chip_exchange(): lax.ppermute(piece, 'tp', [(i, i ^ 2 * k) for i in range(groups)])  7.59 us
    all_to_all x1, starting transfers between devices, gather_queries(): got = lax.all_to_all(split, 'tp', split_axis=1, concat_axis=0, tiled=True)  5.41 us
    pallas_call x1, Pallas kernels, pack_pages(): pl.pallas_call(functools.partial(pack_kernel, capacity), out_shape=jax.Sh...  3.06 us
    all_gather x1, blocking collectives, pair_gather(): return lax.all_gather(x, 'tp', axis=0, tiled=False, axis_index_groups=chips)  1.86 us
    pallas_call x1, Pallas kernels, land_pages(): pl.pallas_call(land_kernel, out_shape=jax.ShapeDtypeStruct(old.shape, old...  1.58 us
  transfers between devices with their start and end apart: 5, of which 4 were waited for; matrix products, arithmetic and copies ran while one was open for 2% of the time, Pallas kernels for 10%

profile of v4, /device:TPU:48, one launch (start us, length us, event | category | flops | bytes accessed | tf_op | source)
XLA Modules:
  0.0 58.3 jit_solution(704922328530982200)
XLA Ops:
  0.6 5.4 %all-to-all-start = ((bf16[2,8,1024]{2,0,1:T(2,128)(2,1)}), bf16[2,8,1024]{2,0,1:T(2,128)(2,1)S(1)}, u32[]{:S(2)}, u32[]{:S(2)}) async-start(bf16[2,8,1024]{2,0,1:T(2,128)(2,1)} %bitcast.36), calls=%async_computation | async-start | bytes 65536 | tf_op jit(solution)/shard_map/all_to_all | solution.py:262
  6.0 3.1 %pack_pages.1 = bf16[128,16,256]{2,1,0:T(8,128)(2,1)} custom-call(s32[1,64]{1,0:T(1,128)} %pages_ref.1, s32[1,64]{1,0:T(1,128)} %bitcast.41, bf16[256,16,256]{2,1,0:T(8,128)(2,1)} %bitcast.33), custom_call_target="tpu_custom_call" | custom-call | tf_op jit(solution)/shard_map/pack_pages/pallas_call | solution.py:64
  9.1 0.0 copy-start
  9.1 0.3 all-to-all-done
  9.4 0.0 copy-start.6
  9.4 15.3 %all-to-all-start.1 = ((bf16[128,16,256]{2,1,0:T(8,128)(2,1)}), bf16[128,16,256]{2,1,0:T(8,128)(2,1)S(1)}, u32[]{:S(2)}, u32[]{:S(2)}) async-start(bf16[128,16,256]{2,1,0:T(8,128)(2,1)} %pack_pages.1), calls=%async_computation.1 | async-start | bytes 2097152 | tf_op jit(solution)/shard_map/all_to_all | solution.py:353
  24.8 0.1 eq.36
  24.8 0.1 lt.56
  24.9 0.1 subtract_clamp_fusion
  25.0 0.1 min.12
  25.1 0.1 select_reduce_fusion
  25.2 0.1 reshape.215
  25.3 0.1 copy.28
  25.4 0.1 copy.30
  25.5 0.1 copy.31
  25.6 0.1 copy.29
  25.7 0.0 copy-start.2
  25.7 0.0 copy-start.3
  25.7 1.1 %attend.1 = bf16[16,1152]{1,0:T(8,128)(2,1)S(1)} custom-call(bf16[16,1024]{1,0:T(8,128)(2,1)S(1)} %reshape.212.query_ref, s32[32,128]{1,0:T(8,128)S(1)} %compare_select_fusion.owner_ref, bf16[4096,256]{1,0:T(8,128)(2,1)S(1)} %bitcast.34), custom_call_target="tpu_custom_call" | custom-call | flops 268435456 | bytes 2097152 | tf_op jit(solution)/shard_map/attend/pallas_call | solution.py:204
  26.9 1.9 %all-gather = bf16[32,1152]{1,0:T(8,128)(2,1)S(1)} all-gather(bf16[16,1152]{1,0:T(8,128)(2,1)S(1)} %attend.1), channel_id=2, replica_groups={{0,1},{2,3},{4,5},{6,7},{8,9},{10,11},{12,13},{14,15},{16,17},{18,19},{..., dimensions={0}, use_global_device_ids=true | all-gather | bytes 110592 | tf_op jit(solution)/shard_map/all_gather | solution.py:244
  28.8 3.4 %collective-permute-start.2 = (bf16[2,2,1152]{2,1,0:T(2,128)(2,1)S(1)}, bf16[2,2,1152]{2,1,0:T(2,128)(2,1)S(1)}, u32[]{:S(2)}, u32[]{:S(2)}) collective-permute-start(bf16[2,2,1152]{2,1,0:T(2,128)(2,1)S(1)} %get-tuple-element.14), channel_id=1, source_target_pairs={{0,6},{1,7},{2,4},{3,5},{4,2},{5,3},{6,0},{7,1},{8,14},{9,15},{10,... | collective-permute-start | bytes 27656 | tf_op jit(solution)/shard_map/ppermute | solution.py:254
  32.2 4.0 %collective-permute-start.1 = (bf16[2,2,1152]{2,1,0:T(2,128)(2,1)S(1)}, bf16[2,2,1152]{2,1,0:T(2,128)(2,1)S(1)}, u32[]{:S(2)}, u32[]{:S(2)}) collective-permute-start(bf16[2,2,1152]{2,1,0:T(2,128)(2,1)S(1)} %get-tuple-element.15), channel_id=1, source_target_pairs={{0,4},{1,5},{2,6},{3,7},{4,0},{5,1},{6,2},{7,3},{8,12},{9,13},{10,... | collective-permute-start | bytes 27656 | tf_op jit(solution)/shard_map/ppermute | solution.py:254
  36.2 2.1 %collective-permute-start = (bf16[2,2,1152]{2,1,0:T(2,128)(2,1)S(1)}, bf16[2,2,1152]{2,1,0:T(2,128)(2,1)S(1)}, u32[]{:S(2)}, u32[]{:S(2)}) collective-permute-start(bf16[2,2,1152]{2,1,0:T(2,128)(2,1)S(1)} %get-tuple-element.16), channel_id=1, source_target_pairs={{0,2},{1,3},{2,0},{3,1},{4,6},{5,7},{6,4},{7,5},{8,10},{9,11},{10,... | collective-permute-start | bytes 27656 | tf_op jit(solution)/shard_map/ppermute | solution.py:254
  38.3 0.1 select_reduce_fusion.1.source_ref
  38.4 0.0 copy-start.1
  38.4 1.2 %copy-done.1 = bf16[1,128,16,1,256]{4,2,3,1,0:T(8,128)(2,1)S(1)} copy-done((bf16[1,128,16,1,256]{4,2,3,1,0:T(8,128)(2,1)S(1)}, bf16[1,128,16,1,256]{4,2,3,1,0:T(8,128)(2,1)}, u32[]{:S(2)}) %copy-start.1) | copy-done | bytes 1048600
  39.7 0.1 stage_old_pages.1.old_ref
  39.7 4.4 %collective-permute-done.2.refs_3_ = bf16[2,2,1152]{2,1,0:T(2,128)(2,1)S(1)} collective-permute-done((bf16[2,2,1152]{2,1,0:T(2,128)(2,1)S(1)}, bf16[2,2,1152]{2,1,0:T(2,128)(2,1)S(1)}, u32[]{:S(2)}, u32[]{:S(2)}) %collective-permute-start.2) | collective-permute-done | bytes 9248 | tf_op jit(solution)/shard_map/ppermute | solution.py:254
  44.1 3.2 %collective-permute-done.refs_1_ = bf16[2,2,1152]{2,1,0:T(2,128)(2,1)S(1)} collective-permute-done((bf16[2,2,1152]{2,1,0:T(2,128)(2,1)S(1)}, bf16[2,2,1152]{2,1,0:T(2,128)(2,1)S(1)}, u32[]{:S(2)}, u32[]{:S(2)}) %collective-permute-start) | collective-permute-done | bytes 9248 | tf_op jit(solution)/shard_map/ppermute | solution.py:254
  47.3 1.6 %add_new_token.1 = bf16[2,8192]{1,0:T(2,128)(2,1)} custom-call(s32[1]{0:T(128)} %bitcast.chip_ref, bf16[2,8192]{1,0:T(2,128)(2,1)S(1)} %copy-done.2, bf16[2,2048]{1,0:T(2,128)(2,1)S(1)} %copy-done.3, bf16[2,2,1152]{2,1,0:T(2,128)(2,1)S(1)} %get-tuple-element.17.refs_0_, bf16[2,2,1152]{2,1,0:T(2,128)(2,1)S(1)} %collective-permute-done.refs_1_, ...), custom_call_target="tpu_custom_call" | custom-call | flops 131072 | bytes 65536 | tf_op jit(solution)/shard_map/add_new_token/pallas_call | solution.py:316
  48.9 7.8 %all-to-all-done.1.arrived_ref = bf16[128,16,256]{2,1,0:T(8,128)(2,1)S(1)} async-done(((bf16[128,16,256]{2,1,0:T(8,128)(2,1)}), bf16[128,16,256]{2,1,0:T(8,128)(2,1)S(1)}, u32[]{:S(2)}, u32[]{:S(2)}) %all-to-all-start.1) | async-done | bytes 1048608 | tf_op jit(solution)/shard_map/all_to_all | solution.py:353
  56.7 1.6 %land_pages.1 = bf16[128,16,256]{2,1,0:T(8,128)(2,1)} custom-call(s32[128]{0:T(128)S(1)} %select_reduce_fusion.1.source_ref, bf16[128,16,256]{2,1,0:T(8,128)(2,1)S(1)} %all-to-all-done.1.arrived_ref, bf16[128,16,256]{2,1,0:T(8,128)(2,1)S(1)} %stage_old_pages.1.old_ref), custom_call_target="tpu_custom_call" | custom-call | tf_op jit(solution)/shard_map/land_pages/pallas_call | solution.py:128
  (20 shorter events, 0.2 us)
Async XLA Ops:
  0.6 8.8 %all-to-all-start = ((bf16[2,8,1024]{2,0,1:T(2,128)(2,1)}), bf16[2,8,1024]{2,0,1:T(2,128)(2,1)S(1)}, u32[]{:S(2)}, u32[]{:S(2)}) async-start(bf16[2,8,1024]{2,0,1:T(2,128)(2,1)} %bitcast.36), calls=%async_computation | async-start | bytes 65536 | tf_op jit(solution)/shard_map/all_to_all | solution.py:262
  6.0 18.7 %copy-start.4 = (s32[16,16]{1,0:T(8,128)S(1)}, s32[16,16]{1,0:T(8,128)}, u32[]{:S(2)}) copy-start(s32[16,16]{1,0:T(8,128)} %param.13) | copy-start | bytes 3076
  6.0 18.9 %copy-start.5 = (s32[16]{0:T(128)S(1)}, s32[16]{0:T(128)}, u32[]{:S(2)}) copy-start(s32[16]{0:T(128)} %param.12) | copy-start | bytes 196
  9.1 16.6 %copy-start = (bf16[1,256,16,1,256]{4,2,3,1,0:T(8,128)(2,1)S(1)}, bf16[1,256,16,1,256]{4,2,3,1,0:T(8,128)(2,1)}, u32[]{:S(2)}) copy-start(bf16[1,256,16,1,256]{4,2,3,1,0:T(8,128)(2,1)} %param.11) | copy-start | bytes 6291460
  9.4 28.9 %copy-start.6 = (s32[1,128]{1,0:T(1,128)S(1)}, s32[1,128]{1,0:T(1,128)}, u32[]{:S(2)}) copy-start(s32[1,128]{1,0:T(1,128)} %param.17) | copy-start | bytes 1540
  9.4 47.3 %all-to-all-start.1 = ((bf16[128,16,256]{2,1,0:T(8,128)(2,1)}), bf16[128,16,256]{2,1,0:T(8,128)(2,1)S(1)}, u32[]{:S(2)}, u32[]{:S(2)}) async-start(bf16[128,16,256]{2,1,0:T(8,128)(2,1)} %pack_pages.1), calls=%async_computation.1 | async-start | bytes 2097152 | tf_op jit(solution)/shard_map/all_to_all | solution.py:353
  25.7 21.7 %copy-start.2 = (bf16[2,8192]{1,0:T(2,128)(2,1)S(1)}, bf16[2,8192]{1,0:T(2,128)(2,1)}, u32[]{:S(2)}) copy-start(bf16[2,8192]{1,0:T(2,128)(2,1)} %query_ref.1) | copy-start | bytes 98308
  25.7 21.7 %copy-start.3 = (bf16[2,2048]{1,0:T(2,128)(2,1)S(1)}, bf16[2,2048]{1,0:T(2,128)(2,1)}, u32[]{:S(2)}) copy-start(bf16[2,2048]{1,0:T(2,128)(2,1)} %fresh_ref.1) | copy-start | bytes 24580
  28.8 15.3 %collective-permute-start.2 = (bf16[2,2,1152]{2,1,0:T(2,128)(2,1)S(1)}, bf16[2,2,1152]{2,1,0:T(2,128)(2,1)S(1)}, u32[]{:S(2)}, u32[]{:S(2)}) collective-permute-start(bf16[2,2,1152]{2,1,0:T(2,128)(2,1)S(1)} %get-tuple-element.14), channel_id=1, source_target_pairs={{0,6},{1,7},{2,4},{3,5},{4,2},{5,3},{6,0},{7,1},{8,14},{9,15},{10,... | collective-permute-start | bytes 27656 | tf_op jit(solution)/shard_map/ppermute | solution.py:254
  32.2 11.9 %collective-permute-start.1 = (bf16[2,2,1152]{2,1,0:T(2,128)(2,1)S(1)}, bf16[2,2,1152]{2,1,0:T(2,128)(2,1)S(1)}, u32[]{:S(2)}, u32[]{:S(2)}) collective-permute-start(bf16[2,2,1152]{2,1,0:T(2,128)(2,1)S(1)} %get-tuple-element.15), channel_id=1, source_target_pairs={{0,4},{1,5},{2,6},{3,7},{4,0},{5,1},{6,2},{7,3},{8,12},{9,13},{10,... | collective-permute-start | bytes 27656 | tf_op jit(solution)/shard_map/ppermute | solution.py:254
  36.2 11.1 %collective-permute-start = (bf16[2,2,1152]{2,1,0:T(2,128)(2,1)S(1)}, bf16[2,2,1152]{2,1,0:T(2,128)(2,1)S(1)}, u32[]{:S(2)}, u32[]{:S(2)}) collective-permute-start(bf16[2,2,1152]{2,1,0:T(2,128)(2,1)S(1)} %get-tuple-element.16), channel_id=1, source_target_pairs={{0,2},{1,3},{2,0},{3,1},{4,6},{5,7},{6,4},{7,5},{8,10},{9,11},{10,... | collective-permute-start | bytes 27656 | tf_op jit(solution)/shard_map/ppermute | solution.py:254
  38.4 1.2 %copy-start.1 = (bf16[1,128,16,1,256]{4,2,3,1,0:T(8,128)(2,1)S(1)}, bf16[1,128,16,1,256]{4,2,3,1,0:T(8,128)(2,1)}, u32[]{:S(2)}) copy-start(bf16[1,128,16,1,256]{4,2,3,1,0:T(8,128)(2,1)} %param.16) | copy-start | bytes 3145732

commit v5 on v4

--- a/solution.py
+++ b/solution.py
@@ -258,9 +258,23 @@
 def gather_queries(queries):
     groups = lax.axis_size("tp")
     rows = queries.shape[0]
-    split = queries.reshape(rows, groups, -1)
-    got = lax.all_to_all(split, "tp", split_axis=1, concat_axis=0, tiled=True)
-    return got.reshape(groups * rows, -1)
+    split = queries.reshape(rows, groups // 2, -1)
+    got = lax.all_to_all(
+        split,
+        "tp",
+        split_axis=1,
+        concat_axis=0,
+        tiled=True,
+        axis_index_groups=[[i for i in range(groups) if i % 2 == core] for core in (0, 1)],
+    )
+    return got.reshape(groups // 2 * rows, -1)
+
+
+def share_queries(part, rows_local, me):
+    rows, width = part.shape
+    both = pair_gather(part).reshape(2, rows // rows_local, rows_local, 2, width // 2)
+    mine = lax.dynamic_index_in_dim(both, me % 2, 3, keepdims=False)
+    return mine.transpose(1, 0, 2, 3).reshape(2 * rows, width // 2)
 
 
 def return_heads(mixed, me):
@@ -356,6 +370,7 @@
 
     owner = token_owners(context_lens, block_table, pages, page_size)
     scale = dim ** (-0.5)
+    query = share_queries(query, queries.shape[0], me)
     mixed = attend(query, owner, pool.reshape(pages * page_size, width), scale)
     returned = return_heads(mixed, me)
     attended = add_new_token(returned, queries, new_kv, dim, scale)

time: 58.8 us -> 58.1 us (0.988)
  waiting for transfers between devices: 15.7 us -> 13 us
  blocking collectives: 1.86 us -> 3.71 us
    ppermute x3, waiting for transfers between devices: 7.59 us -> 4.73 us  [chip_exchange(): lax.ppermute(piece, 'tp', [(i, i ^ 2 * k) for i in range(groups)])]
    all_gather x1 -> x2, blocking collectives: 1.86 us -> 3.71 us  [pair_gather(): return lax.all_gather(x, 'tp', axis=0, tiled=False, axis_index_groups=chips)]
  transfers between devices with their start and end apart: 5 -> 5, of which waited for: 4 -> 3; matrix products, arithmetic and copies ran while one was open for 2% -> 2% of each run, Pallas kernels for 10% -> 10%
where the time goes in v5:
time: 58.1 us; the launch traced here: 57.6 us
  starting transfers between devices  30 us (52%)
  waiting for transfers between devices  13 us (22%)
  Pallas kernels  7.45 us (13%)
  blocking collectives  3.71 us (6%)
  local copies, waits for them, and re-layouts  2.12 us (4%)
  between operations  0.91 us (2%)
    all_to_all x1, starting transfers between devices, on_device(): lax.all_to_all(outgoing, 'inst', split_axis=0, concat_axis=0, tiled=True,...  15.3 us
    ppermute x3, starting transfers between devices, chip_exchange(): lax.ppermute(piece, 'tp', [(i, i ^ 2 * k) for i in range(groups)])  9.34 us
    all_to_all x1, waiting for transfers between devices, on_device(): lax.all_to_all(outgoing, 'inst', split_axis=0, concat_axis=0, tiled=True,...  7.96 us
    all_to_all x1, starting transfers between devices, gather_queries(): lax.all_to_all(split, 'tp', split_axis=1, concat_axis=0, tiled=True, axis...  5.38 us
    ppermute x3, waiting for transfers between devices, chip_exchange(): lax.ppermute(piece, 'tp', [(i, i ^ 2 * k) for i in range(groups)])  4.73 us
    all_gather x2, blocking collectives, pair_gather(): return lax.all_gather(x, 'tp', axis=0, tiled=False, axis_index_groups=chips)  3.71 us
    pallas_call x1, Pallas kernels, pack_pages(): pl.pallas_call(functools.partial(pack_kernel, capacity), out_shape=jax.Sh...  3.06 us
    pallas_call x1, Pallas kernels, land_pages(): pl.pallas_call(land_kernel, out_shape=jax.ShapeDtypeStruct(old.shape, old...  1.58 us
  transfers between devices with their start and end apart: 5, of which 3 were waited for; matrix products, arithmetic and copies ran while one was open for 2% of the time, Pallas kernels for 10%

profile of v5, /device:TPU:48, one launch (start us, length us, event | category | flops | bytes accessed | tf_op | source)
XLA Modules:
  0.0 57.6 jit_solution(17149240984533597392)
XLA Ops:
  0.6 5.4 %all-to-all-start = ((bf16[2,4,2048]{2,0,1:T(2,128)(2,1)}), bf16[2,4,2048]{2,0,1:T(2,128)(2,1)S(1)}, u32[]{:S(2)}, u32[]{:S(2)}) async-start(bf16[2,4,2048]{2,0,1:T(2,128)(2,1)} %bitcast.42), calls=%async_computation | async-start | bytes 65536 | tf_op jit(solution)/shard_map/all_to_all | solution.py:262
  6.0 3.1 %pack_pages.1 = bf16[128,16,256]{2,1,0:T(8,128)(2,1)} custom-call(s32[1,64]{1,0:T(1,128)} %pages_ref.1, s32[1,64]{1,0:T(1,128)} %bitcast.48, bf16[256,16,256]{2,1,0:T(8,128)(2,1)} %bitcast.39), custom_call_target="tpu_custom_call" | custom-call | tf_op jit(solution)/shard_map/pack_pages/pallas_call | solution.py:64
  9.1 0.0 copy-start
  9.1 0.3 all-to-all-done
  9.4 15.3 %all-to-all-start.1 = ((bf16[128,16,256]{2,1,0:T(8,128)(2,1)}), bf16[128,16,256]{2,1,0:T(8,128)(2,1)S(1)}, u32[]{:S(2)}, u32[]{:S(2)}) async-start(bf16[128,16,256]{2,1,0:T(8,128)(2,1)} %pack_pages.1), calls=%async_computation.1 | async-start | bytes 2097152 | tf_op jit(solution)/shard_map/all_to_all | solution.py:367
  24.8 0.1 eq.37
  24.9 0.1 lt.62
  25.0 0.1 subtract_clamp_fusion
  25.0 0.1 min.12
  25.1 0.1 select_reduce_fusion
  25.3 0.1 reshape.223
  25.4 0.1 copy.39
  25.4 0.1 copy.41
  25.5 0.1 copy.42
  25.6 0.1 copy.40
  25.7 1.9 %all-gather = bf16[16,2048]{1,0:T(8,128)(2,1)S(1)} all-gather(bf16[8,2048]{1,0:T(8,128)(2,1)S(1)} %reshape.218), channel_id=2, replica_groups={{0,1},{2,3},{4,5},{6,7},{8,9},{10,11},{12,13},{14,15},{16,17},{18,19},{..., dimensions={0}, use_global_device_ids=true | all-gather | bytes 98304 | tf_op jit(solution)/shard_map/all_gather | solution.py:244
  27.6 0.1 constant_dynamic-slice_fusion
  27.8 0.0 copy-start.2
  27.8 0.0 copy-start.3
  27.8 1.2 %attend.1 = bf16[16,1152]{1,0:T(8,128)(2,1)S(1)} custom-call(bf16[16,1024]{1,0:T(8,128)(2,1)S(1)} %reshape.222.query_ref, s32[32,128]{1,0:T(8,128)S(1)} %compare_select_fusion.owner_ref, bf16[4096,256]{1,0:T(8,128)(2,1)S(1)} %bitcast.40), custom_call_target="tpu_custom_call" | custom-call | flops 268435456 | bytes 2097152 | tf_op jit(solution)/shard_map/attend/pallas_call | solution.py:204
  28.9 1.9 %all-gather.1 = bf16[32,1152]{1,0:T(8,128)(2,1)S(1)} all-gather(bf16[16,1152]{1,0:T(8,128)(2,1)S(1)} %attend.1), channel_id=3, replica_groups={{0,1},{2,3},{4,5},{6,7},{8,9},{10,11},{12,13},{14,15},{16,17},{18,19},{..., dimensions={0}, use_global_device_ids=true | all-gather | bytes 110592 | tf_op jit(solution)/shard_map/all_gather | solution.py:244
  30.9 3.3 %collective-permute-start.2 = (bf16[2,2,1152]{2,1,0:T(2,128)(2,1)S(1)}, bf16[2,2,1152]{2,1,0:T(2,128)(2,1)S(1)}, u32[]{:S(2)}, u32[]{:S(2)}) collective-permute-start(bf16[2,2,1152]{2,1,0:T(2,128)(2,1)S(1)} %get-tuple-element.16), channel_id=1, source_target_pairs={{0,6},{1,7},{2,4},{3,5},{4,2},{5,3},{6,0},{7,1},{8,14},{9,15},{10,... | collective-permute-start | bytes 27656 | tf_op jit(solution)/shard_map/ppermute | solution.py:254
  34.2 4.0 %collective-permute-start.1 = (bf16[2,2,1152]{2,1,0:T(2,128)(2,1)S(1)}, bf16[2,2,1152]{2,1,0:T(2,128)(2,1)S(1)}, u32[]{:S(2)}, u32[]{:S(2)}) collective-permute-start(bf16[2,2,1152]{2,1,0:T(2,128)(2,1)S(1)} %get-tuple-element.17), channel_id=1, source_target_pairs={{0,4},{1,5},{2,6},{3,7},{4,0},{5,1},{6,2},{7,3},{8,12},{9,13},{10,... | collective-permute-start | bytes 27656 | tf_op jit(solution)/shard_map/ppermute | solution.py:254
  38.3 2.0 %collective-permute-start = (bf16[2,2,1152]{2,1,0:T(2,128)(2,1)S(1)}, bf16[2,2,1152]{2,1,0:T(2,128)(2,1)S(1)}, u32[]{:S(2)}, u32[]{:S(2)}) collective-permute-start(bf16[2,2,1152]{2,1,0:T(2,128)(2,1)S(1)} %get-tuple-element.18), channel_id=1, source_target_pairs={{0,2},{1,3},{2,0},{3,1},{4,6},{5,7},{6,4},{7,5},{8,10},{9,11},{10,... | collective-permute-start | bytes 27656 | tf_op jit(solution)/shard_map/ppermute | solution.py:254
  40.3 0.1 select_reduce_fusion.1.source_ref
  40.4 0.0 copy-start.1
  40.4 1.2 %copy-done.1 = bf16[1,128,16,1,256]{4,2,3,1,0:T(8,128)(2,1)S(1)} copy-done((bf16[1,128,16,1,256]{4,2,3,1,0:T(8,128)(2,1)S(1)}, bf16[1,128,16,1,256]{4,2,3,1,0:T(8,128)(2,1)}, u32[]{:S(2)}) %copy-start.1) | copy-done | bytes 1048600
  41.6 0.1 stage_old_pages.1.old_ref
  41.7 4.7 %collective-permute-done.refs_1_ = bf16[2,2,1152]{2,1,0:T(2,128)(2,1)S(1)} collective-permute-done((bf16[2,2,1152]{2,1,0:T(2,128)(2,1)S(1)}, bf16[2,2,1152]{2,1,0:T(2,128)(2,1)S(1)}, u32[]{:S(2)}, u32[]{:S(2)}) %collective-permute-start) | collective-permute-done | bytes 9248 | tf_op jit(solution)/shard_map/ppermute | solution.py:254
  46.4 1.6 %add_new_token.1 = bf16[2,8192]{1,0:T(2,128)(2,1)} custom-call(s32[1]{0:T(128)} %bitcast.chip_ref, bf16[2,8192]{1,0:T(2,128)(2,1)S(1)} %copy-done.2, bf16[2,2048]{1,0:T(2,128)(2,1)S(1)} %copy-done.3, bf16[2,2,1152]{2,1,0:T(2,128)(2,1)S(1)} %get-tuple-element.19.refs_0_, bf16[2,2,1152]{2,1,0:T(2,128)(2,1)S(1)} %collective-permute-done.refs_1_, ...), custom_call_target="tpu_custom_call" | custom-call | flops 131072 | bytes 65536 | tf_op jit(solution)/shard_map/add_new_token/pallas_call | solution.py:330
  48.0 8.0 %all-to-all-done.1.arrived_ref = bf16[128,16,256]{2,1,0:T(8,128)(2,1)S(1)} async-done(((bf16[128,16,256]{2,1,0:T(8,128)(2,1)}), bf16[128,16,256]{2,1,0:T(8,128)(2,1)S(1)}, u32[]{:S(2)}, u32[]{:S(2)}) %all-to-all-start.1) | async-done | bytes 1048608 | tf_op jit(solution)/shard_map/all_to_all | solution.py:367
  56.0 1.6 %land_pages.1 = bf16[128,16,256]{2,1,0:T(8,128)(2,1)} custom-call(s32[128]{0:T(128)S(1)} %select_reduce_fusion.1.source_ref, bf16[128,16,256]{2,1,0:T(8,128)(2,1)S(1)} %all-to-all-done.1.arrived_ref, bf16[128,16,256]{2,1,0:T(8,128)(2,1)S(1)} %stage_old_pages.1.old_ref), custom_call_target="tpu_custom_call" | custom-call | tf_op jit(solution)/shard_map/land_pages/pallas_call | solution.py:128
  (25 shorter events, 0.3 us)
Async XLA Ops:
  0.6 8.8 %all-to-all-start = ((bf16[2,4,2048]{2,0,1:T(2,128)(2,1)}), bf16[2,4,2048]{2,0,1:T(2,128)(2,1)S(1)}, u32[]{:S(2)}, u32[]{:S(2)}) async-start(bf16[2,4,2048]{2,0,1:T(2,128)(2,1)} %bitcast.42), calls=%async_computation | async-start | bytes 65536 | tf_op jit(solution)/shard_map/all_to_all | solution.py:262
  6.0 18.8 %copy-start.4 = (s32[16,16]{1,0:T(8,128)S(1)}, s32[16,16]{1,0:T(8,128)}, u32[]{:S(2)}) copy-start(s32[16,16]{1,0:T(8,128)} %param.13) | copy-start | bytes 3076
  6.0 18.9 %copy-start.5 = (s32[16]{0:T(128)S(1)}, s32[16]{0:T(128)}, u32[]{:S(2)}) copy-start(s32[16]{0:T(128)} %param.12) | copy-start | bytes 196
  9.1 18.7 %copy-start = (bf16[1,256,16,1,256]{4,2,3,1,0:T(8,128)(2,1)S(1)}, bf16[1,256,16,1,256]{4,2,3,1,0:T(8,128)(2,1)}, u32[]{:S(2)}) copy-start(bf16[1,256,16,1,256]{4,2,3,1,0:T(8,128)(2,1)} %param.11) | copy-start | bytes 6291460
  9.4 46.6 %all-to-all-start.1 = ((bf16[128,16,256]{2,1,0:T(8,128)(2,1)}), bf16[128,16,256]{2,1,0:T(8,128)(2,1)S(1)}, u32[]{:S(2)}, u32[]{:S(2)}) async-start(bf16[128,16,256]{2,1,0:T(8,128)(2,1)} %pack_pages.1), calls=%async_computation.1 | async-start | bytes 2097152 | tf_op jit(solution)/shard_map/all_to_all | solution.py:367
  24.7 15.5 %copy-start.6 = (s32[1,128]{1,0:T(1,128)S(1)}, s32[1,128]{1,0:T(1,128)}, u32[]{:S(2)}) copy-start(s32[1,128]{1,0:T(1,128)} %param.17) | copy-start | bytes 1540
  27.8 18.7 %copy-start.2 = (bf16[2,8192]{1,0:T(2,128)(2,1)S(1)}, bf16[2,8192]{1,0:T(2,128)(2,1)}, u32[]{:S(2)}) copy-start(bf16[2,8192]{1,0:T(2,128)(2,1)} %query_ref.1) | copy-start | bytes 98308
  27.8 18.7 %copy-start.3 = (bf16[2,2048]{1,0:T(2,128)(2,1)S(1)}, bf16[2,2048]{1,0:T(2,128)(2,1)}, u32[]{:S(2)}) copy-start(bf16[2,2048]{1,0:T(2,128)(2,1)} %fresh_ref.1) | copy-start | bytes 24580
  30.9 10.8 %collective-permute-start.2 = (bf16[2,2,1152]{2,1,0:T(2,128)(2,1)S(1)}, bf16[2,2,1152]{2,1,0:T(2,128)(2,1)S(1)}, u32[]{:S(2)}, u32[]{:S(2)}) collective-permute-start(bf16[2,2,1152]{2,1,0:T(2,128)(2,1)S(1)} %get-tuple-element.16), channel_id=1, source_target_pairs={{0,6},{1,7},{2,4},{3,5},{4,2},{5,3},{6,0},{7,1},{8,14},{9,15},{10,... | collective-permute-start | bytes 27656 | tf_op jit(solution)/shard_map/ppermute | solution.py:254
  34.2 7.5 %collective-permute-start.1 = (bf16[2,2,1152]{2,1,0:T(2,128)(2,1)S(1)}, bf16[2,2,1152]{2,1,0:T(2,128)(2,1)S(1)}, u32[]{:S(2)}, u32[]{:S(2)}) collective-permute-start(bf16[2,2,1152]{2,1,0:T(2,128)(2,1)S(1)} %get-tuple-element.17), channel_id=1, source_target_pairs={{0,4},{1,5},{2,6},{3,7},{4,0},{5,1},{6,2},{7,3},{8,12},{9,13},{10,... | collective-permute-start | bytes 27656 | tf_op jit(solution)/shard_map/ppermute | solution.py:254
  38.3 8.2 %collective-permute-start = (bf16[2,2,1152]{2,1,0:T(2,128)(2,1)S(1)}, bf16[2,2,1152]{2,1,0:T(2,128)(2,1)S(1)}, u32[]{:S(2)}, u32[]{:S(2)}) collective-permute-start(bf16[2,2,1152]{2,1,0:T(2,128)(2,1)S(1)} %get-tuple-element.18), channel_id=1, source_target_pairs={{0,2},{1,3},{2,0},{3,1},{4,6},{5,7},{6,4},{7,5},{8,10},{9,11},{10,... | collective-permute-start | bytes 27656 | tf_op jit(solution)/shard_map/ppermute | solution.py:254
  40.4 1.2 %copy-start.1 = (bf16[1,128,16,1,256]{4,2,3,1,0:T(8,128)(2,1)S(1)}, bf16[1,128,16,1,256]{4,2,3,1,0:T(8,128)(2,1)}, u32[]{:S(2)}) copy-start(bf16[1,128,16,1,256]{4,2,3,1,0:T(8,128)(2,1)} %param.16) | copy-start | bytes 3145732

commit v6 on v5

--- a/solution.py
+++ b/solution.py
@@ -136,7 +136,7 @@
         out_specs=pl.BlockSpec(memory_space=pl.ANY),
         scratch_shapes=[
             pltpu.VMEM(old.shape, old.dtype),
-            pltpu.SemaphoreType.DMA((8,)),
+            pltpu.SemaphoreType.DMA((4,)),
         ],
         compiler_params=pltpu.CompilerParams(vmem_limit_bytes=16 * 1024 * 1024),
         name="land_pages",

time: 58.1 us -> 58 us (level)
  no operation moved by 1% of the time
where the time goes in v6:
time: 58 us; the launch traced here: 57.5 us
  starting transfers between devices  30 us (52%)
  waiting for transfers between devices  13 us (22%)
  Pallas kernels  7.44 us (13%)
  blocking collectives  3.71 us (6%)
  local copies, waits for them, and re-layouts  2.12 us (4%)
  between operations  0.91 us (2%)
    all_to_all x1, starting transfers between devices, on_device(): lax.all_to_all(outgoing, 'inst', split_axis=0, concat_axis=0, tiled=True,...  15.3 us
    ppermute x3, starting transfers between devices, chip_exchange(): lax.ppermute(piece, 'tp', [(i, i ^ 2 * k) for i in range(groups)])  9.34 us
    all_to_all x1, waiting for transfers between devices, on_device(): lax.all_to_all(outgoing, 'inst', split_axis=0, concat_axis=0, tiled=True,...  7.96 us
    all_to_all x1, starting transfers between devices, gather_queries(): lax.all_to_all(split, 'tp', split_axis=1, concat_axis=0, tiled=True, axis...  5.38 us
    ppermute x3, waiting for transfers between devices, chip_exchange(): lax.ppermute(piece, 'tp', [(i, i ^ 2 * k) for i in range(groups)])  4.73 us
    all_gather x2, blocking collectives, pair_gather(): return lax.all_gather(x, 'tp', axis=0, tiled=False, axis_index_groups=chips)  3.71 us
    pallas_call x1, Pallas kernels, pack_pages(): pl.pallas_call(functools.partial(pack_kernel, capacity), out_shape=jax.Sh...  3.06 us
    pallas_call x1, Pallas kernels, land_pages(): pl.pallas_call(land_kernel, out_shape=jax.ShapeDtypeStruct(old.shape, old...  1.58 us
  transfers between devices with their start and end apart: 5, of which 3 were waited for; matrix products, arithmetic and copies ran while one was open for 2% of the time, Pallas kernels for 10%

profile of v6, /device:TPU:48, one launch (start us, length us, event | category | flops | bytes accessed | tf_op | source)
XLA Modules:
  0.0 57.5 jit_solution(16685825041465968606)
XLA Ops:
  0.6 5.4 %all-to-all-start = ((bf16[2,4,2048]{2,0,1:T(2,128)(2,1)}), bf16[2,4,2048]{2,0,1:T(2,128)(2,1)S(1)}, u32[]{:S(2)}, u32[]{:S(2)}) async-start(bf16[2,4,2048]{2,0,1:T(2,128)(2,1)} %bitcast.42), calls=%async_computation | async-start | bytes 65536 | tf_op jit(solution)/shard_map/all_to_all | solution.py:262
  6.0 3.1 %pack_pages.1 = bf16[128,16,256]{2,1,0:T(8,128)(2,1)} custom-call(s32[1,64]{1,0:T(1,128)} %pages_ref.1, s32[1,64]{1,0:T(1,128)} %bitcast.48, bf16[256,16,256]{2,1,0:T(8,128)(2,1)} %bitcast.39), custom_call_target="tpu_custom_call" | custom-call | tf_op jit(solution)/shard_map/pack_pages/pallas_call | solution.py:64
  9.1 0.0 copy-start
  9.1 0.3 all-to-all-done
  9.4 15.3 %all-to-all-start.1 = ((bf16[128,16,256]{2,1,0:T(8,128)(2,1)}), bf16[128,16,256]{2,1,0:T(8,128)(2,1)S(1)}, u32[]{:S(2)}, u32[]{:S(2)}) async-start(bf16[128,16,256]{2,1,0:T(8,128)(2,1)} %pack_pages.1), calls=%async_computation.1 | async-start | bytes 2097152 | tf_op jit(solution)/shard_map/all_to_all | solution.py:367
  24.7 0.0 copy-start.6
  24.8 0.1 eq.37
  24.9 0.1 lt.62
  25.0 0.1 subtract_clamp_fusion
  25.0 0.1 min.12
  25.1 0.1 select_reduce_fusion
  25.3 0.1 reshape.223
  25.4 0.1 copy.39
  25.4 0.1 copy.41
  25.5 0.1 copy.42
  25.6 0.1 copy.40
  25.7 1.9 %all-gather = bf16[16,2048]{1,0:T(8,128)(2,1)S(1)} all-gather(bf16[8,2048]{1,0:T(8,128)(2,1)S(1)} %reshape.218), channel_id=2, replica_groups={{0,1},{2,3},{4,5},{6,7},{8,9},{10,11},{12,13},{14,15},{16,17},{18,19},{..., dimensions={0}, use_global_device_ids=true | all-gather | bytes 98304 | tf_op jit(solution)/shard_map/all_gather | solution.py:244
  27.6 0.1 constant_dynamic-slice_fusion
  27.8 0.0 copy-start.2
  27.8 0.0 copy-start.3
  27.8 1.2 %attend.1 = bf16[16,1152]{1,0:T(8,128)(2,1)S(1)} custom-call(bf16[16,1024]{1,0:T(8,128)(2,1)S(1)} %reshape.222.query_ref, s32[32,128]{1,0:T(8,128)S(1)} %compare_select_fusion.owner_ref, bf16[4096,256]{1,0:T(8,128)(2,1)S(1)} %bitcast.40), custom_call_target="tpu_custom_call" | custom-call | flops 268435456 | bytes 2097152 | tf_op jit(solution)/shard_map/attend/pallas_call | solution.py:204
  28.9 1.9 %all-gather.1 = bf16[32,1152]{1,0:T(8,128)(2,1)S(1)} all-gather(bf16[16,1152]{1,0:T(8,128)(2,1)S(1)} %attend.1), channel_id=3, replica_groups={{0,1},{2,3},{4,5},{6,7},{8,9},{10,11},{12,13},{14,15},{16,17},{18,19},{..., dimensions={0}, use_global_device_ids=true | all-gather | bytes 110592 | tf_op jit(solution)/shard_map/all_gather | solution.py:244
  30.9 3.3 %collective-permute-start.2 = (bf16[2,2,1152]{2,1,0:T(2,128)(2,1)S(1)}, bf16[2,2,1152]{2,1,0:T(2,128)(2,1)S(1)}, u32[]{:S(2)}, u32[]{:S(2)}) collective-permute-start(bf16[2,2,1152]{2,1,0:T(2,128)(2,1)S(1)} %get-tuple-element.16), channel_id=1, source_target_pairs={{0,6},{1,7},{2,4},{3,5},{4,2},{5,3},{6,0},{7,1},{8,14},{9,15},{10,... | collective-permute-start | bytes 27656 | tf_op jit(solution)/shard_map/ppermute | solution.py:254
  34.2 4.0 %collective-permute-start.1 = (bf16[2,2,1152]{2,1,0:T(2,128)(2,1)S(1)}, bf16[2,2,1152]{2,1,0:T(2,128)(2,1)S(1)}, u32[]{:S(2)}, u32[]{:S(2)}) collective-permute-start(bf16[2,2,1152]{2,1,0:T(2,128)(2,1)S(1)} %get-tuple-element.17), channel_id=1, source_target_pairs={{0,4},{1,5},{2,6},{3,7},{4,0},{5,1},{6,2},{7,3},{8,12},{9,13},{10,... | collective-permute-start | bytes 27656 | tf_op jit(solution)/shard_map/ppermute | solution.py:254
  38.3 2.0 %collective-permute-start = (bf16[2,2,1152]{2,1,0:T(2,128)(2,1)S(1)}, bf16[2,2,1152]{2,1,0:T(2,128)(2,1)S(1)}, u32[]{:S(2)}, u32[]{:S(2)}) collective-permute-start(bf16[2,2,1152]{2,1,0:T(2,128)(2,1)S(1)} %get-tuple-element.18), channel_id=1, source_target_pairs={{0,2},{1,3},{2,0},{3,1},{4,6},{5,7},{6,4},{7,5},{8,10},{9,11},{10,... | collective-permute-start | bytes 27656 | tf_op jit(solution)/shard_map/ppermute | solution.py:254
  40.3 0.1 select_reduce_fusion.1.source_ref
  40.4 1.2 %copy-done.1 = bf16[1,128,16,1,256]{4,2,3,1,0:T(8,128)(2,1)S(1)} copy-done((bf16[1,128,16,1,256]{4,2,3,1,0:T(8,128)(2,1)S(1)}, bf16[1,128,16,1,256]{4,2,3,1,0:T(8,128)(2,1)}, u32[]{:S(2)}) %copy-start.1) | copy-done | bytes 1048600
  41.6 0.1 stage_old_pages.1.old_ref
  41.7 4.7 %collective-permute-done.refs_1_ = bf16[2,2,1152]{2,1,0:T(2,128)(2,1)S(1)} collective-permute-done((bf16[2,2,1152]{2,1,0:T(2,128)(2,1)S(1)}, bf16[2,2,1152]{2,1,0:T(2,128)(2,1)S(1)}, u32[]{:S(2)}, u32[]{:S(2)}) %collective-permute-start) | collective-permute-done | bytes 9248 | tf_op jit(solution)/shard_map/ppermute | solution.py:254
  46.4 1.6 %add_new_token.1 = bf16[2,8192]{1,0:T(2,128)(2,1)} custom-call(s32[1]{0:T(128)} %bitcast.chip_ref, bf16[2,8192]{1,0:T(2,128)(2,1)S(1)} %copy-done.2, bf16[2,2048]{1,0:T(2,128)(2,1)S(1)} %copy-done.3, bf16[2,2,1152]{2,1,0:T(2,128)(2,1)S(1)} %get-tuple-element.19.refs_0_, bf16[2,2,1152]{2,1,0:T(2,128)(2,1)S(1)} %collective-permute-done.refs_1_, ...), custom_call_target="tpu_custom_call" | custom-call | flops 131072 | bytes 65536 | tf_op jit(solution)/shard_map/add_new_token/pallas_call | solution.py:330
  48.0 8.0 %all-to-all-done.1.arrived_ref = bf16[128,16,256]{2,1,0:T(8,128)(2,1)S(1)} async-done(((bf16[128,16,256]{2,1,0:T(8,128)(2,1)}), bf16[128,16,256]{2,1,0:T(8,128)(2,1)S(1)}, u32[]{:S(2)}, u32[]{:S(2)}) %all-to-all-start.1) | async-done | bytes 1048608 | tf_op jit(solution)/shard_map/all_to_all | solution.py:367
  56.0 1.6 %land_pages.1 = bf16[128,16,256]{2,1,0:T(8,128)(2,1)} custom-call(s32[128]{0:T(128)S(1)} %select_reduce_fusion.1.source_ref, bf16[128,16,256]{2,1,0:T(8,128)(2,1)S(1)} %all-to-all-done.1.arrived_ref, bf16[128,16,256]{2,1,0:T(8,128)(2,1)S(1)} %stage_old_pages.1.old_ref), custom_call_target="tpu_custom_call" | custom-call | tf_op jit(solution)/shard_map/land_pages/pallas_call | solution.py:128
  (25 shorter events, 0.3 us)
Async XLA Ops:
  0.6 8.8 %all-to-all-start = ((bf16[2,4,2048]{2,0,1:T(2,128)(2,1)}), bf16[2,4,2048]{2,0,1:T(2,128)(2,1)S(1)}, u32[]{:S(2)}, u32[]{:S(2)}) async-start(bf16[2,4,2048]{2,0,1:T(2,128)(2,1)} %bitcast.42), calls=%async_computation | async-start | bytes 65536 | tf_op jit(solution)/shard_map/all_to_all | solution.py:262
  6.0 18.8 %copy-start.4 = (s32[16,16]{1,0:T(8,128)S(1)}, s32[16,16]{1,0:T(8,128)}, u32[]{:S(2)}) copy-start(s32[16,16]{1,0:T(8,128)} %param.13) | copy-start | bytes 3076
  6.0 18.9 %copy-start.5 = (s32[16]{0:T(128)S(1)}, s32[16]{0:T(128)}, u32[]{:S(2)}) copy-start(s32[16]{0:T(128)} %param.12) | copy-start | bytes 196
  9.1 18.7 %copy-start = (bf16[1,256,16,1,256]{4,2,3,1,0:T(8,128)(2,1)S(1)}, bf16[1,256,16,1,256]{4,2,3,1,0:T(8,128)(2,1)}, u32[]{:S(2)}) copy-start(bf16[1,256,16,1,256]{4,2,3,1,0:T(8,128)(2,1)} %param.11) | copy-start | bytes 6291460
  9.4 46.6 %all-to-all-start.1 = ((bf16[128,16,256]{2,1,0:T(8,128)(2,1)}), bf16[128,16,256]{2,1,0:T(8,128)(2,1)S(1)}, u32[]{:S(2)}, u32[]{:S(2)}) async-start(bf16[128,16,256]{2,1,0:T(8,128)(2,1)} %pack_pages.1), calls=%async_computation.1 | async-start | bytes 2097152 | tf_op jit(solution)/shard_map/all_to_all | solution.py:367
  24.7 15.5 %copy-start.6 = (s32[1,128]{1,0:T(1,128)S(1)}, s32[1,128]{1,0:T(1,128)}, u32[]{:S(2)}) copy-start(s32[1,128]{1,0:T(1,128)} %param.17) | copy-start | bytes 1540
  27.8 18.7 %copy-start.2 = (bf16[2,8192]{1,0:T(2,128)(2,1)S(1)}, bf16[2,8192]{1,0:T(2,128)(2,1)}, u32[]{:S(2)}) copy-start(bf16[2,8192]{1,0:T(2,128)(2,1)} %query_ref.1) | copy-start | bytes 98308
  27.8 18.7 %copy-start.3 = (bf16[2,2048]{1,0:T(2,128)(2,1)S(1)}, bf16[2,2048]{1,0:T(2,128)(2,1)}, u32[]{:S(2)}) copy-start(bf16[2,2048]{1,0:T(2,128)(2,1)} %fresh_ref.1) | copy-start | bytes 24580
  30.9 10.8 %collective-permute-start.2 = (bf16[2,2,1152]{2,1,0:T(2,128)(2,1)S(1)}, bf16[2,2,1152]{2,1,0:T(2,128)(2,1)S(1)}, u32[]{:S(2)}, u32[]{:S(2)}) collective-permute-start(bf16[2,2,1152]{2,1,0:T(2,128)(2,1)S(1)} %get-tuple-element.16), channel_id=1, source_target_pairs={{0,6},{1,7},{2,4},{3,5},{4,2},{5,3},{6,0},{7,1},{8,14},{9,15},{10,... | collective-permute-start | bytes 27656 | tf_op jit(solution)/shard_map/ppermute | solution.py:254
  34.2 7.5 %collective-permute-start.1 = (bf16[2,2,1152]{2,1,0:T(2,128)(2,1)S(1)}, bf16[2,2,1152]{2,1,0:T(2,128)(2,1)S(1)}, u32[]{:S(2)}, u32[]{:S(2)}) collective-permute-start(bf16[2,2,1152]{2,1,0:T(2,128)(2,1)S(1)} %get-tuple-element.17), channel_id=1, source_target_pairs={{0,4},{1,5},{2,6},{3,7},{4,0},{5,1},{6,2},{7,3},{8,12},{9,13},{10,... | collective-permute-start | bytes 27656 | tf_op jit(solution)/shard_map/ppermute | solution.py:254
  38.3 8.2 %collective-permute-start = (bf16[2,2,1152]{2,1,0:T(2,128)(2,1)S(1)}, bf16[2,2,1152]{2,1,0:T(2,128)(2,1)S(1)}, u32[]{:S(2)}, u32[]{:S(2)}) collective-permute-start(bf16[2,2,1152]{2,1,0:T(2,128)(2,1)S(1)} %get-tuple-element.18), channel_id=1, source_target_pairs={{0,2},{1,3},{2,0},{3,1},{4,6},{5,7},{6,4},{7,5},{8,10},{9,11},{10,... | collective-permute-start | bytes 27656 | tf_op jit(solution)/shard_map/ppermute | solution.py:254
  40.4 1.2 %copy-start.1 = (bf16[1,128,16,1,256]{4,2,3,1,0:T(8,128)(2,1)S(1)}, bf16[1,128,16,1,256]{4,2,3,1,0:T(8,128)(2,1)}, u32[]{:S(2)}) copy-start(bf16[1,128,16,1,256]{4,2,3,1,0:T(8,128)(2,1)} %param.16) | copy-start | bytes 3145732
